TPU v7x, 128 devices: a whole 4x4x4 slice. The times are simulated.
128 devices in a mesh: gx: 32 (over y, x, core), sp: 4 (over z).
Axes of the slice: x: 4, y: 4, z: 4, core: 2. Of those that a mesh axis runs over, the one named last changes fastest.
Arguments:
- previous_head: float32 [8, 256, 512], P(None, 'gx', 'sp'), may hold values from -6 to 6
- recharge: float32 [8, 256, 512], P(None, 'gx', 'sp'), may hold values from -6 to 6
- soil_zone: int32 [8, 256, 512], P(None, 'gx', 'sp'), may hold values from 0 to 7
- soil_cond: float32 [8], replicated, may hold values from 0.1 to 1
- soil_store: float32 [8], replicated, may hold values from 0.05 to 0.5
- species: float32 [12, 8, 256, 512], P('sp', None, 'gx'), may hold values from -6 to 6
- mineral_zone: int32 [8, 256, 512], P(None, 'gx', 'sp'), may hold values from 0 to 5
- rate_table: float32 [6, 8], replicated, may hold values from 0.3 to 3
- stoich: float32 [12, 8], replicated, may hold values from -3 to 3
- log_equil: float32 [8], replicated, may hold values from -1 to 1
Outputs:
- head_field: float32 [8, 256, 512], P(None, 'gx', 'sp')
- species_out: float32 [12, 8, 256, 512], P('sp', None, 'gx')
Inputs may be any that keep to these rules, and one draw needn't show every extreme that they name: `soil_zone`: a soil class of 8. `mineral_zone`: a mineral zone class of 6.
All inputs are finite; a program needn't handle non-finite values.
Results may differ from a plain program's by a relative error of at most 0.0003.
Values sent between devices are 32-bit elements; how exact they have to be, the bound alone decides.
A program may use at most 64 MiB of HBM per device.

v0:
```python
import jax
import jax.numpy as jnp
from jax import lax
from jax.sharding import PartitionSpec as P

ITERS = 6
NEWTON = 2


time_step = 0.05
dispersion = 0.5
reaction_span = 0.5
newton_damping = 0.5


def padded_2(cells, sides, width):
    for axis, dim in sides:
        count = lax.axis_size(axis)
        ends = count - 1
        head = lax.slice_in_dim(cells, 0, width, axis=dim)
        tail = lax.slice_in_dim(cells, cells.shape[dim] - width, cells.shape[dim], axis=dim)
        cells = jnp.concatenate(
            [
                lax.ppermute(tail, axis, [(i, (i + 1) % count) for i in range(ends)]),
                cells,
                lax.ppermute(head, axis, [((i + 1) % count, i) for i in range(ends)]),
            ],
            axis=dim,
        )
    return cells


def harmonic(center, other):
    return 2.0 * center * other / (center + other)


def six_sides(padded):
    return [
        padded[..., 2:, 1:-1, 1:-1],
        padded[..., :-2, 1:-1, 1:-1],
        padded[..., 1:-1, 2:, 1:-1],
        padded[..., 1:-1, :-2, 1:-1],
        padded[..., 1:-1, 1:-1, 2:],
        padded[..., 1:-1, 1:-1, :-2],
    ]


def lookup(labels, entries):
    levels = jnp.arange(entries.shape[0], dtype=jnp.int32).reshape((-1,) + (1,) * labels.ndim)
    return jnp.sum(jnp.where(labels[None] == levels, entries.reshape(levels.shape), 0.0), axis=0)


def lookup_rows(labels, entries):
    levels = jnp.arange(entries.shape[0], dtype=jnp.int32)[:, None, None]
    return jnp.sum(jnp.where(labels[None, None, :] == levels, entries[:, :, None], 0.0), axis=0)


def transport(concentration, conc_padded, head_padded, cond_padded):
    head_center = head_padded[1:-1, 1:-1, 1:-1]
    conduct = cond_padded[1:-1, 1:-1, 1:-1]
    change = jnp.zeros_like(concentration)
    for beside, head_beside, cond_beside in zip(
        six_sides(conc_padded), six_sides(head_padded), six_sides(cond_padded)
    ):
        face_cond = harmonic(conduct, cond_beside)
        velocity = face_cond * (head_center - head_beside)
        change = (
            change
            + jnp.maximum(velocity, 0.0) * concentration
            + jnp.minimum(velocity, 0.0) * beside
        )
        change = change + dispersion * face_cond * (concentration - beside)
    return concentration - time_step * change


def solve_system(jacobian, mismatch):
    dimension = mismatch.shape[0]
    factor = [[None] * dimension for i in range(dimension)]
    inverse = [None] * dimension
    for j in range(dimension):
        for i in range(j, dimension):
            running = jacobian[i * dimension + j] + (1.0 if i == j else 0.0)
            for k in range(j):
                running = running - factor[i][k] * factor[j][k]
            if i == j:
                diag_root = jnp.sqrt(running)
                factor[j][j] = diag_root
                inverse[j] = 1.0 / diag_root
            else:
                factor[i][j] = running * inverse[j]
    forward = []
    for i in range(dimension):
        running = mismatch[i]
        for k in range(i):
            running = running - factor[i][k] * forward[k]
        forward.append(running * inverse[i])
    answer = [None] * dimension
    for i in reversed(range(dimension)):
        running = forward[i]
        for k in range(i + 1, dimension):
            running = running - factor[k][i] * answer[k]
        answer[i] = running * inverse[i]
    return jnp.stack(answer, 0)


def reaction(concentration, labels, rate_table, stoich, log_equil):
    rate_cells = lookup_rows(labels, rate_table)
    pair_products = (stoich[:, None, :] * stoich[None, :, :]).reshape(-1, stoich.shape[1])
    iterate = concentration
    for newton_pass in range(NEWTON):
        affinity = (
            jnp.dot(
                stoich.T,
                iterate,
                precision=lax.Precision.HIGHEST,
                preferred_element_type=jnp.float32,
            )
            - log_equil[:, None]
        )
        tangent = jnp.tanh(affinity)
        mismatch = (
            iterate
            - concentration
            + reaction_span
            * jnp.dot(
                stoich,
                rate_cells * tangent,
                precision=lax.Precision.HIGHEST,
                preferred_element_type=jnp.float32,
            )
        )
        jacobian = reaction_span * jnp.dot(
            pair_products,
            rate_cells * (1.0 - tangent * tangent),
            precision=lax.Precision.HIGHEST,
            preferred_element_type=jnp.float32,
        )
        iterate = iterate - newton_damping * solve_system(jacobian, mismatch)
    return iterate


def pad_vertical(field):
    return jnp.pad(field, ((1, 1), (0, 0), (0, 0)))


def to_cells(block):
    return lax.all_to_all(block, "sp", split_axis=3, concat_axis=0, tiled=True)


def residual_squares(residual):
    return lax.psum(jnp.sum(residual * residual), ("gx", "sp"))


def per_device(
    previous_head,
    recharge,
    soil_zone,
    soil_cond,
    soil_store,
    species,
    mineral_zone,
    rate_table,
    stoich,
    log_equil,
):
    conduct = lookup(soil_zone, soil_cond)
    storage = lookup(soil_zone, soil_store)
    cond_padded = pad_vertical(padded_2(conduct, (("gx", 1), ("sp", 2)), 1))
    faces = [harmonic(conduct, beside) for beside in six_sides(cond_padded)]
    source = storage * previous_head + recharge
    head_field = jnp.zeros_like(source)
    residual = source
    direction = source
    norm_now = residual_squares(residual)
    for iteration in range(ITERS):
        operate_padded = pad_vertical(padded_2(direction, (("gx", 1), ("sp", 2)), 1))
        result = storage * direction
        for face_cond, operate_beside in zip(faces, six_sides(operate_padded)):
            result = result + face_cond * (direction - operate_beside)
        alpha = norm_now / lax.psum(jnp.sum(direction * result), ("gx", "sp"))
        head_field = head_field + alpha * direction
        residual = residual - alpha * result
        norm_next = residual_squares(residual)
        direction = residual + norm_next / norm_now * direction
        norm_now = norm_next
    head_rows, cond_rows = (
        lax.all_gather(head_field, "sp", axis=2, tiled=True),
        lax.all_gather(conduct, "sp", axis=2, tiled=True),
    )
    stacked = jnp.concatenate([species, head_rows[None], cond_rows[None]], 0)
    padded = padded_2(stacked, (("gx", 2),), 1)
    padded = jnp.pad(padded, ((0, 0), (1, 1), (0, 0), (1, 1)))
    moved = transport(species, padded[:-2], padded[-2], padded[-1])
    cells = to_cells(moved)
    block_shape = cells.shape
    reacted = reaction(
        cells.reshape(block_shape[0], -1), mineral_zone.reshape(-1), rate_table, stoich, log_equil
    )
    reacted = reacted.reshape(block_shape)
    species_out = lax.all_to_all(reacted, "sp", split_axis=0, concat_axis=3, tiled=True)
    return (head_field, species_out)


def solution(mesh):
    in_specs = (
        P(None, "gx", "sp"),
        P(None, "gx", "sp"),
        P(None, "gx", "sp"),
        P(),
        P(),
        P("sp", None, "gx", None),
        P(None, "gx", "sp"),
        P(),
        P(),
        P(),
    )
    out_specs = (P(None, "gx", "sp"), P("sp", None, "gx", None))
    return jax.shard_map(
        per_device, mesh=mesh, in_specs=in_specs, out_specs=out_specs, check_vma=False
    )
```

profile of v0, /device:TPU:1, one launch (start us, length us, event | category | flops | bytes accessed | tf_op | source)
XLA Modules:
  0.0 961.9 jit_solution(2798620576376435652)
XLA Ops:
  1.5 3.3 collective-permute-start.1
  4.9 3.1 collective-permute-start
  13.2 3.5 collective-permute-start.2
  19.5 4.8 collective-permute-start.6
  26.9 71.5 %all-reduce.8 = (f32[]{:T(128)}, f32[]{:T(128)}) all-reduce(f32[]{:T(128)} %get-tuple-element.5, f32[]{:T(128)} %get-tuple-element.4), channel_id=1, replica_groups=mesh['gx'=32,'sp'=4] {'gx','sp'}, use_global_device_ids=true, to_apply=%region_2.3 | all-reduce | flops 2 | bytes 16 | tf_op jit(solution)/shard_map/psum | solution.py:151
  100.4 62.5 %psum.86 = f32[]{:T(128)} all-reduce(f32[]{:T(128)} %multiply_reduce_fusion.8), channel_id=1, replica_groups=mesh['gx'=32,'sp'=4] {'gx','sp'}, use_global_device_ids=true, to_apply=%region_7.8 | all-reduce | flops 1 | bytes 8 | tf_op jit(solution)/shard_map/psum | solution.py:151
  164.3 3.5 collective-permute-start.8
  169.8 3.0 collective-permute-done.9
  174.2 4.0 collective-permute-start.10
  180.4 66.2 %psum.87 = f32[]{:T(128)} all-reduce(f32[]{:T(128)} %get-tuple-element.204), channel_id=1, replica_groups=mesh['gx'=32,'sp'=4] {'gx','sp'}, use_global_device_ids=true, to_apply=%region_9.10 | all-reduce | flops 1 | bytes 8 | tf_op jit(solution)/shard_map/psum | solution.py:180
  248.5 63.8 %psum.88 = f32[]{:T(128)} all-reduce(f32[]{:T(128)} %get-tuple-element.202), channel_id=1, replica_groups=mesh['gx'=32,'sp'=4] {'gx','sp'}, use_global_device_ids=true, to_apply=%region_11.12 | all-reduce | flops 1 | bytes 8 | tf_op jit(solution)/shard_map/psum | solution.py:151
  318.1 2.5 collective-permute-done.13
  322.0 4.1 collective-permute-start.14
  328.3 67.6 %psum.89 = f32[]{:T(128)} all-reduce(f32[]{:T(128)} %get-tuple-element.200), channel_id=1, replica_groups=mesh['gx'=32,'sp'=4] {'gx','sp'}, use_global_device_ids=true, to_apply=%region_13.14 | all-reduce | flops 1 | bytes 8 | tf_op jit(solution)/shard_map/psum | solution.py:180
  397.9 62.6 %psum.90 = f32[]{:T(128)} all-reduce(f32[]{:T(128)} %get-tuple-element.198), channel_id=1, replica_groups=mesh['gx'=32,'sp'=4] {'gx','sp'}, use_global_device_ids=true, to_apply=%region_15.16 | all-reduce | flops 1 | bytes 8 | tf_op jit(solution)/shard_map/psum | solution.py:151
  461.8 3.5 collective-permute-start.16
  467.3 3.0 collective-permute-done.17
  471.7 4.0 collective-permute-start.18
  477.9 66.6 %psum.91 = f32[]{:T(128)} all-reduce(f32[]{:T(128)} %get-tuple-element.196), channel_id=1, replica_groups=mesh['gx'=32,'sp'=4] {'gx','sp'}, use_global_device_ids=true, to_apply=%region_17.18 | all-reduce | flops 1 | bytes 8 | tf_op jit(solution)/shard_map/psum | solution.py:180
  546.5 64.3 %psum.92 = f32[]{:T(128)} all-reduce(f32[]{:T(128)} %get-tuple-element.194), channel_id=1, replica_groups=mesh['gx'=32,'sp'=4] {'gx','sp'}, use_global_device_ids=true, to_apply=%region_19.20 | all-reduce | flops 1 | bytes 8 | tf_op jit(solution)/shard_map/psum | solution.py:151
  616.5 2.5 collective-permute-done.21
  620.4 4.0 collective-permute-start.22
  626.6 67.2 %psum.93 = f32[]{:T(128)} all-reduce(f32[]{:T(128)} %get-tuple-element.192), channel_id=1, replica_groups=mesh['gx'=32,'sp'=4] {'gx','sp'}, use_global_device_ids=true, to_apply=%region_21.22 | all-reduce | flops 1 | bytes 8 | tf_op jit(solution)/shard_map/psum | solution.py:180
  695.8 62.7 %psum.94 = f32[]{:T(128)} all-reduce(f32[]{:T(128)} %multiply_reduce_fusion), channel_id=1, replica_groups=mesh['gx'=32,'sp'=4] {'gx','sp'}, use_global_device_ids=true, to_apply=%region_23.24 | all-reduce | flops 1 | bytes 8 | tf_op jit(solution)/shard_map/psum | solution.py:151
  759.8 3.5 collective-permute-start.24
  765.3 3.0 collective-permute-done.25
  769.7 4.0 collective-permute-start.26
  775.9 9.5 all_gather.7
  785.4 68.0 %psum.95 = f32[]{:T(128)} all-reduce(f32[]{:T(128)} %fusion.320), channel_id=1, replica_groups=mesh['gx'=32,'sp'=4] {'gx','sp'}, use_global_device_ids=true, to_apply=%region_25.26 | all-reduce | flops 1 | bytes 8 | tf_op jit(solution)/shard_map/psum | solution.py:180
  854.7 9.1 all_gather.6
  864.0 4.6 collective-permute-start.28
  868.6 2.7 collective-permute-start.29
  871.4 2.9 collective-permute-done.29
  877.4 4.2 copy.54
  881.6 6.1 reshape.95
  887.7 4.2 all-to-all-start
  892.3 6.0 all-to-all-done
  900.6 6.2 reshape.96
  906.8 4.3 copy.55
  912.4 3.9 convolution_multiply_fusion.1
  916.3 7.2 subtract_multiply_fusion.64
  923.5 3.0 subtract_multiply_fusion.57
  926.5 4.1 subtract_multiply_fusion.46
  932.4 3.9 convolution_multiply_fusion
  936.3 7.3 subtract_multiply_fusion.18
  943.6 2.7 subtract_multiply_fusion.11
  946.4 4.1 subtract_multiply_fusion
  950.9 10.0 %all_to_all.33 = f32[12,8,8,128]{3,2,1,0:T(8,128)S(1)} all-to-all(f32[12,8,8,128]{3,2,1,0:T(8,128)S(1)} %fusion.11), channel_id=1, replica_groups=mesh['gx'=32,'sp'=4] {'sp'}, dimensions={0} | all-to-all | bytes 786432 | tf_op jit(solution)/shard_map/all_to_all | solution.py:200
  (147 shorter events, 56.8 us)
Async XLA Ops:
  1.5 11.6 %collective-permute-start.1 = (f32[8,1,128]{2,1,0:T(1,128)S(1)}, f32[8,1,128]{2,1,0:T(1,128)S(1)}, u32[]{:S(2)}, u32[]{:S(2)}) collective-permute-start(f32[8,1,128]{2,1,0:T(1,128)S(1)} %get-tuple-element.257), channel_id=1, source_target_pairs={{4,0},{8,4},{12,8},{16,12},{20,16},{24,20},{28,24},{32,28},{36,32}... | collective-permute-start | bytes 12296 | tf_op jit(solution)/shard_map/ppermute | solution.py:26
  4.9 8.3 collective-permute-start
  8.8 9.3 collective-permute-start.4
  11.2 6.9 collective-permute-start.5
  13.2 11.1 %collective-permute-start.2 = (f32[8,10,1]{2,1,0:T(8,128)S(1)}, f32[8,10,1]{2,1,0:T(8,128)S(1)}, u32[]{:S(2)}, u32[]{:S(2)}) collective-permute-start(f32[8,10,1]{2,1,0:T(8,128)S(1)} %get-tuple-element.243), channel_id=1, source_target_pairs={{0,1},{1,2},{2,3},{4,5},{5,6},{6,7},{8,9},{9,10},{10,11},{12,13},{... | collective-permute-start | bytes 968 | tf_op jit(solution)/shard_map/ppermute | solution.py:24
  16.8 7.5 collective-permute-start.3
  18.2 6.7 collective-permute-start.7
  19.5 6.5 collective-permute-start.6
  164.3 5.5 collective-permute-start.8
  167.9 4.9 collective-permute-start.9
  172.9 5.3 collective-permute-start.11
  174.2 5.3 collective-permute-start.10
  313.7 4.3 collective-permute-start.12
  315.7 4.9 collective-permute-start.13
  320.7 5.4 collective-permute-start.15
  322.0 451.7 %copy-start = (f32[3,8,8,512]{3,2,1,0:T(8,128)S(1)}, f32[3,8,8,512]{3,2,1,0:T(8,128)}, u32[]{:S(2)}) copy-start(f32[3,8,8,512]{3,2,1,0:T(8,128)} %param.15) | copy-start | bytes 1179652
  322.0 5.4 collective-permute-start.14
  461.8 5.5 collective-permute-start.16
  465.4 4.9 collective-permute-start.17
  470.4 5.3 collective-permute-start.19
  471.7 5.3 collective-permute-start.18
  612.2 4.3 collective-permute-start.20
  614.1 4.9 collective-permute-start.21
  619.1 5.3 collective-permute-start.23
  620.4 5.3 collective-permute-start.22
  625.9 245.5 %copy-start.3 = (s32[8,8,128]{2,1,0:T(8,128)S(1)}, s32[8,8,128]{2,1,0:T(8,128)}, u32[]{:S(2)}) copy-start(s32[8,8,128]{2,1,0:T(8,128)} %param.16) | copy-start | bytes 98308
  759.8 5.4 collective-permute-start.24
  763.3 4.9 collective-permute-start.25
  768.4 5.5 collective-permute-start.27
  769.7 5.3 collective-permute-start.26
  854.7 20.4 %copy-start.2 = (f32[8,8,128]{2,1,0:T(8,128)}, f32[8,8,128]{2,1,0:T(8,128)S(1)}, u32[]{:S(2)}) copy-start(f32[8,8,128]{2,1,0:T(8,128)S(1)} %multiply_add_fusion) | copy-start | bytes 98308
  864.0 7.4 collective-permute-start.28
  868.6 5.8 collective-permute-start.29
  881.6 10.2 %copy-start.1 = (f32[12,8]{0,1:T(8,128)S(1)}, f32[12,8]{0,1:T(8,128)}, u32[]{:S(2)}) copy-start(f32[12,8]{0,1:T(8,128)} %param.18) | copy-start | bytes 1156
  881.6 10.4 %copy-start.4 = (f32[6,8]{1,0:T(8,128)S(1)}, f32[6,8]{1,0:T(8,128)}, u32[]{:S(2)}) copy-start(f32[6,8]{1,0:T(8,128)} %param.17) | copy-start | bytes 580
  887.7 10.7 %all-to-all-start = ((f32[4,1,24576]{2,1,0:T(1,128)}), f32[4,1,24576]{2,1,0:T(1,128)S(1)}, u32[]{:S(2)}, u32[]{:S(2)}) async-start(f32[4,1,24576]{2,1,0:T(1,128)} %reshape.95), calls=%async_computation | async-start | bytes 786432 | tf_op jit(solution)/shard_map/all_to_all | solution.py:147
  906.8 4.4 copy-start.5
where the time goes:
time: 974 us; the launch traced here: 962 us
  blocking collectives  752 us (77%)
  starting transfers between devices  84.6 us (9%)
  other arithmetic  44.1 us (5%)
  waiting for transfers between devices  30.7 us (3%)
  local copies, waits for them, and re-layouts  24.1 us (2%)
  between operations  16.6 us (2%)
  matrix products  10.1 us (1%)
    psum x6, blocking collectives, residual_squares(): return lax.psum(jnp.sum(residual * residual), ('gx', 'sp'))  387 us
    psum x5, blocking collectives, per_device(): alpha = norm_now / lax.psum(jnp.sum(direction * result), ('gx', 'sp'))  336 us
    ppermute x15, starting transfers between devices, padded_2(): lax.ppermute(tail, axis, [(i, (i + 1) % count) for i in range(ends)])  52.9 us
    ppermute x15, starting transfers between devices, padded_2(): lax.ppermute(head, axis, [((i + 1) % count, i) for i in range(ends)])  27.6 us
  transfers between devices with their start and end apart: 31, of which 14 were waited for; matrix products, arithmetic and copies ran while one was open for 0% of the time, Pallas kernels for 0%

commit v1 on v0

--- a/solution.py
+++ b/solution.py
@@ -1,16 +1,336 @@
+import functools
+
 import jax
 import jax.numpy as jnp
 from jax import lax
+from jax.experimental import pallas as pl
+from jax.experimental.pallas import tpu as pltpu
 from jax.sharding import PartitionSpec as P
 
-ITERS = 6
 NEWTON = 2
-
+BLOCK = 3
 
 time_step = 0.05
 dispersion = 0.5
 reaction_span = 0.5
 newton_damping = 0.5
+
+MESH = pl.DeviceIdType.MESH
+EXACT = lax.Precision.HIGHEST
+
+
+def table_lookup(labels, table):
+    found = jnp.full(labels.shape, table[0], jnp.float32)
+    for level in range(1, table.shape[0]):
+        found = jnp.where(labels == level, table[level], found)
+    return found
+
+
+def harmonic_safe(center, other):
+    return 2.0 * center * other / jnp.maximum(center + other, 1e-30)
+
+
+def shifted(field, offset, axis):
+    size = field.shape[axis]
+    return pltpu.roll(field, (-offset) % size, axis)
+
+
+def layer_above(field):
+    return jnp.concatenate([field[1:], field[-1:]], axis=0)
+
+
+def layer_below(field):
+    return jnp.concatenate([field[:1], field[:-1]], axis=0)
+
+
+def six_faces(conduct):
+    east = harmonic_safe(conduct, shifted(conduct, 1, 2))
+    south = harmonic_safe(conduct, shifted(conduct, 1, 1))
+    top = harmonic_safe(conduct[:-1], conduct[1:])
+    none = jnp.zeros_like(conduct[:1])
+    return (
+        jnp.concatenate([top, none], axis=0),
+        jnp.concatenate([none, top], axis=0),
+        south,
+        shifted(south, -1, 1),
+        east,
+        shifted(east, -1, 2),
+    )
+
+
+def six_beside(field):
+    return (
+        layer_above(field),
+        layer_below(field),
+        shifted(field, 1, 1),
+        shifted(field, -1, 1),
+        shifted(field, 1, 2),
+        shifted(field, -1, 2),
+    )
+
+
+def apply_flow(field, storage, faces):
+    result = storage * field
+    for face, beside in zip(faces, six_beside(field)):
+        result = result + face * (field - beside)
+    return result
+
+
+def add_scaled(left, scale, right):
+    total = dict(left)
+    for key, value in right.items():
+        term = scale * value
+        total[key] = total[key] + term if key in total else term
+    return total
+
+
+def cg_block(rr, pr, pp, least, most, same):
+    one = jnp.ones_like(least)
+    direction = {(0, 0): one}
+    residual = {(0 if same else 1, 0): one}
+    change = {}
+    live = None
+    for step in range(BLOCK):
+        alpha = (pr if step == 0 else rr)[0] / jnp.maximum(pp[1], 1e-30)
+        alpha = jnp.clip(alpha, least, most)
+        if live is not None:
+            alpha = jnp.where(live, alpha, 0.0)
+        change = add_scaled(change, alpha, direction)
+        image = {(part, power + 1): value for (part, power), value in direction.items()}
+        residual = add_scaled(residual, -alpha, image)
+        if len(pp) < 3 or len(pr) < 2:
+            break
+        square = alpha * alpha
+        count = min(len(rr), len(pr) - 1, len(pp) - 2)
+        next_rr = [rr[k] - 2.0 * alpha * pr[k + 1] + square * pp[k + 2] for k in range(count)]
+        count = min(len(pr), len(pp) - 1)
+        next_pr = [pr[k] - alpha * pp[k + 1] for k in range(count)]
+        above = next_rr[0] > 1e-6 * (rr[0] + square * pp[2])
+        live = above if live is None else live & above
+        beta = jnp.where(live, next_rr[0] / jnp.maximum(rr[0], 1e-37), 0.0)
+        direction = add_scaled(residual, beta, direction)
+        count = min(len(next_rr), len(next_pr))
+        next_pp = [
+            next_rr[k] + 2.0 * beta * next_pr[k] + beta * beta * pp[k] for k in range(count)
+        ]
+        pr = [next_rr[k] + beta * next_pr[k] for k in range(count)]
+        rr, pp = next_rr, next_pp
+    return change, residual, direction
+
+
+def combine(polynomial, parts):
+    total = None
+    for (part, power), value in sorted(polynomial.items()):
+        term = value[None] * parts[part][power]
+        total = term if total is None else total + term
+    return total
+
+
+def flow_kernel(
+    gx_count,
+    sp_count,
+    inner,
+    previous_head,
+    recharge,
+    soil_zone,
+    soil_cond,
+    soil_store,
+    head_out,
+    field,
+    rows_in,
+    edge_out,
+    edge_in,
+    near_0,
+    far_0,
+    near_1,
+    far_1,
+    halo_send,
+    halo_recv,
+    sum_send,
+    sum_recv,
+):
+    g = lax.axis_index("gx")
+    s = lax.axis_index("sp")
+    outer = gx_count // inner
+    low, high = g % inner, g // inner
+    plane = high * sp_count + s
+    near_peers = [(high * inner + (low + k) % inner, s) for k in range(1, inner)]
+    far_peers = [
+        (((high + k // sp_count) % outer) * inner + low, (s + k % sp_count) % sp_count)
+        for k in range(1, outer * sp_count)
+    ]
+
+    def beside(rows, columns):
+        return ((g + rows + gx_count) % gx_count, (s + columns + sp_count) % sp_count)
+
+    offsets = [(rows, columns) for rows in (-1, 0, 1) for columns in (-1, 0, 1) if (rows, columns) != (0, 0)]
+    barrier = pltpu.get_barrier_semaphore()
+    peers = [beside(*offset) for offset in offsets] + near_peers + far_peers
+    for peer in peers:
+        pl.semaphore_signal(barrier, inc=1, device_id=peer, device_id_type=MESH)
+
+    zone = soil_zone[...]
+    field[0] = table_lookup(zone, soil_store) * previous_head[...] + recharge[...]
+    field[1] = zone.astype(jnp.float32)
+    line = lax.broadcasted_iota(jnp.int32, (16, 128), 0)
+    lane = lax.broadcasted_iota(jnp.int32, (16, 128), 1)
+    pick = (lane == jnp.where(line < 8, line, line + 112)).astype(jnp.float32)
+    edge_out[...] = lax.dot_general(
+        pick,
+        field[...].reshape(128, 128),
+        (((1,), (1,)), ((), ())),
+        precision=EXACT,
+        preferred_element_type=jnp.float32,
+    )
+
+    pl.semaphore_wait(barrier, len(peers))
+    halo = []
+    for number, (rows, columns) in enumerate(offsets):
+        if columns == 0:
+            source, target = field, rows_in.at[0 if rows == 1 else 1]
+        else:
+            first = 8 if columns == 1 else 0
+            source = edge_out.at[pl.ds(first, 8)]
+            target = edge_in.at[1 - rows, pl.ds(first, 8)]
+        copy = pltpu.make_async_remote_copy(
+            src_ref=source,
+            dst_ref=target,
+            send_sem=halo_send.at[number],
+            recv_sem=halo_recv.at[number],
+            device_id=beside(rows, columns),
+            device_id_type=MESH,
+        )
+        copy.start()
+        halo.append(copy)
+    for copy in halo:
+        copy.wait_recv()
+
+    row_blocks = []
+    for block, center in enumerate((rows_in[0], field[...], rows_in[1])):
+        side = lax.dot_general(
+            edge_in[block],
+            pick,
+            (((0,), (0,)), ((), ())),
+            precision=EXACT,
+            preferred_element_type=jnp.float32,
+        ).reshape(2, 8, 8, 128)
+        row_blocks.append(jnp.concatenate([center, side], axis=3))
+    wide = jnp.concatenate(row_blocks, axis=2)
+    row = lax.broadcasted_iota(jnp.int32, (24, 256), 0)
+    column = lax.broadcasted_iota(jnp.int32, (24, 256), 1)
+    first_row = jnp.where(g > 0, 0, 8)
+    end_row = jnp.where(g < gx_count - 1, 24, 16)
+    end_right = jnp.where(s < sp_count - 1, 136, 128)
+    first_left = jnp.where(s > 0, 248, 256)
+    inside = (
+        (row >= first_row)
+        & (row < end_row)
+        & ((column < end_right) | (column >= first_left))
+    )[None]
+    source = jnp.where(inside, wide[0], 0.0)
+    conduct = jnp.where(inside, table_lookup(wide[1], soil_cond), 0.0)
+    storage = jnp.where(inside, table_lookup(wide[1], soil_store), 0.0)
+    faces = six_faces(conduct)
+
+    store_least, store_most, cond_most = soil_store[0], soil_store[0], soil_cond[0]
+    for level in range(1, soil_store.shape[0]):
+        store_least = jnp.minimum(store_least, soil_store[level])
+        store_most = jnp.maximum(store_most, soil_store[level])
+        cond_most = jnp.maximum(cond_most, soil_cond[level])
+    most = 1.0 / jnp.full((1, 256), store_least, jnp.float32)
+    least = 1.0 / jnp.full((1, 256), store_most + 12.0 * cond_most, jnp.float32)
+
+    sends = []
+
+    def exchange(buffer, slot, mine, others, number):
+        buffer[slot] = mine
+        for peer in others:
+            copy = pltpu.make_async_remote_copy(
+                src_ref=buffer.at[slot],
+                dst_ref=buffer.at[slot],
+                send_sem=sum_send.at[number],
+                recv_sem=sum_recv.at[number],
+                device_id=peer,
+                device_id_type=MESH,
+            )
+            copy.start()
+        all_others = buffer.at[pl.ds(0, len(others))]
+        pltpu.make_async_copy(all_others, all_others, sum_recv.at[number]).wait()
+        sends.append(pltpu.make_async_copy(all_others, all_others, sum_send.at[number]))
+        return jnp.sum(buffer[...], axis=0)
+
+    def global_sums(pairs, near, far, number):
+        lines = near.shape[1]
+        index = lax.broadcasted_iota(jnp.int32, (lines, 128), 0)
+        partial = jnp.zeros((lines, 128), jnp.float32)
+        for position, (left, right) in enumerate(pairs):
+            product = left[:, 8:16, :128] * right[:, 8:16, :128]
+            total = jnp.sum(jnp.sum(product, axis=0), axis=0, keepdims=True)
+            partial = jnp.where(index == position, total, partial)
+        partial = exchange(near, low, partial, near_peers, number)
+        partial = exchange(far, plane, partial, far_peers, number + 1)
+        totals = jnp.broadcast_to(jnp.sum(partial, axis=1, keepdims=True), (lines, 256))
+        return [totals[k : k + 1] for k in range(len(pairs))]
+
+    powers = [source]
+    for k in range(BLOCK):
+        powers.append(apply_flow(powers[-1], storage, faces))
+    pairs = [(powers[k // 2], powers[(k + 1) // 2]) for k in range(2 * BLOCK + 1)]
+    moments = global_sums(pairs, near_0, far_0, 0)
+    change, residual, direction = cg_block(moments, moments, moments, least, most, True)
+    head = combine(change, [powers])
+    residual = combine(residual, [powers])
+    direction = combine(direction, [powers])
+
+    p_powers = [direction]
+    for k in range(BLOCK):
+        p_powers.append(apply_flow(p_powers[-1], storage, faces))
+    r_powers = [residual]
+    for k in range(BLOCK - 1):
+        r_powers.append(apply_flow(r_powers[-1], storage, faces))
+    pairs = [(r_powers[k // 2], r_powers[(k + 1) // 2]) for k in range(4)]
+    pairs += [(p_powers[(k + 1) // 2], r_powers[k // 2]) for k in range(5)]
+    pairs += [(p_powers[k // 2], p_powers[(k + 1) // 2]) for k in range(6)]
+    moments = global_sums(pairs, near_1, far_1, 2)
+    change, _, _ = cg_block(moments[:4], moments[4:9], moments[9:], least, most, False)
+    head = head + combine(change, [p_powers, r_powers])
+    head_out[...] = head[:, 8:16, :128]
+
+    for copy in halo:
+        copy.wait_send()
+    for copy in sends:
+        copy.wait()
+
+
+def solve_flow(mesh, previous_head, recharge, soil_zone, soil_cond, soil_store):
+    gx_count, sp_count = mesh.shape["gx"], mesh.shape["sp"]
+    inner = min(8, gx_count // 2)
+    far_count = gx_count // inner * sp_count
+    vmem = pl.BlockSpec(memory_space=pltpu.VMEM)
+    smem = pl.BlockSpec(memory_space=pltpu.SMEM)
+    return pl.pallas_call(
+        functools.partial(flow_kernel, gx_count, sp_count, inner),
+        out_shape=jax.ShapeDtypeStruct((8, 8, 128), jnp.float32),
+        in_specs=[vmem, vmem, vmem, smem, smem],
+        out_specs=vmem,
+        scratch_shapes=[
+            pltpu.VMEM((2, 8, 8, 128), jnp.float32),
+            pltpu.VMEM((2, 2, 8, 8, 128), jnp.float32),
+            pltpu.VMEM((16, 128), jnp.float32),
+            pltpu.VMEM((3, 16, 128), jnp.float32),
+            pltpu.VMEM((inner, 8, 128), jnp.float32),
+            pltpu.VMEM((far_count, 8, 128), jnp.float32),
+            pltpu.VMEM((inner, 16, 128), jnp.float32),
+            pltpu.VMEM((far_count, 16, 128), jnp.float32),
+            pltpu.SemaphoreType.DMA((8,)),
+            pltpu.SemaphoreType.DMA((8,)),
+            pltpu.SemaphoreType.DMA((4,)),
+            pltpu.SemaphoreType.DMA((4,)),
+        ],
+        compiler_params=pltpu.CompilerParams(
+            collective_id=0, has_side_effects=True, vmem_limit_bytes=48 * 1024 * 1024
+        ),
+    )(previous_head, recharge, soil_zone, soil_cond, soil_store)
 
 
 def padded_2(cells, sides, width):
@@ -147,11 +467,8 @@
     return lax.all_to_all(block, "sp", split_axis=3, concat_axis=0, tiled=True)
 
 
-def residual_squares(residual):
-    return lax.psum(jnp.sum(residual * residual), ("gx", "sp"))
-
-
 def per_device(
+    mesh,
     previous_head,
     recharge,
     soil_zone,
@@ -164,25 +481,7 @@
     log_equil,
 ):
     conduct = lookup(soil_zone, soil_cond)
-    storage = lookup(soil_zone, soil_store)
-    cond_padded = pad_vertical(padded_2(conduct, (("gx", 1), ("sp", 2)), 1))
-    faces = [harmonic(conduct, beside) for beside in six_sides(cond_padded)]
-    source = storage * previous_head + recharge
-    head_field = jnp.zeros_like(source)
-    residual = source
-    direction = source
-    norm_now = residual_squares(residual)
-    for iteration in range(ITERS):
-        operate_padded = pad_vertical(padded_2(direction, (("gx", 1), ("sp", 2)), 1))
-        result = storage * direction
-        for face_cond, operate_beside in zip(faces, six_sides(operate_padded)):
-            result = result + face_cond * (direction - operate_beside)
-        alpha = norm_now / lax.psum(jnp.sum(direction * result), ("gx", "sp"))
-        head_field = head_field + alpha * direction
-        residual = residual - alpha * result
-        norm_next = residual_squares(residual)
-        direction = residual + norm_next / norm_now * direction
-        norm_now = norm_next
+    head_field = solve_flow(mesh, previous_head, recharge, soil_zone, soil_cond, soil_store)
     head_rows, cond_rows = (
         lax.all_gather(head_field, "sp", axis=2, tiled=True),
         lax.all_gather(conduct, "sp", axis=2, tiled=True),
@@ -216,5 +515,5 @@
     )
     out_specs = (P(None, "gx", "sp"), P("sp", None, "gx", None))
     return jax.shard_map(
-        per_device, mesh=mesh, in_specs=in_specs, out_specs=out_specs, check_vma=False
-    )
+        functools.partial(per_device, mesh), mesh=mesh, in_specs=in_specs, out_specs=out_specs, check_vma=False
+    )

time: 974 us -> 161 us (0.17)
  blocking collectives: 752 us -> 30.6 us
  starting transfers between devices: 84.6 us -> 11.5 us
  Pallas kernels: 0 us -> 32.6 us
  waiting for transfers between devices: 30.7 us -> 9.31 us
  between operations: 16.6 us -> 1.11 us
    psum x11 -> x0, blocking collectives: 723 us -> none  [the longest x6 387 us: residual_squares(): return lax.psum(jnp.sum(residual * residual), ('gx', 'sp'))]
    ppermute x15 -> x1, starting transfers between devices: 52.9 us -> 5.94 us  [padded_2(): lax.ppermute(tail, axis, [(i, (i + 1) % count) for i in range(ends)])]
    pallas_call x0 -> x1, Pallas kernels: none -> 32.6 us  [solve_flow(): pl.pallas_call(functools.partial(flow_kernel, gx_count, sp_count, inner),...]
    ppermute x15 -> x1, starting transfers between devices: 27.6 us -> 1.92 us  [padded_2(): lax.ppermute(head, axis, [((i + 1) % count, i) for i in range(ends)])]
    ppermute x15 -> x1, waiting for transfers between devices: 17.3 us -> 3.76 us  [padded_2(): lax.ppermute(head, axis, [((i + 1) % count, i) for i in range(ends)])]
  transfers between devices with their start and end apart: 31 -> 3, of which waited for: 14 -> 2; matrix products, arithmetic and copies ran while one was open for 0% -> 0% of each run, Pallas kernels for 0% -> 0%
where the time goes in v1:
time: 161 us; the launch traced here: 159 us
  other arithmetic  34.6 us (21%)
  Pallas kernels  32.6 us (20%)
  blocking collectives  30.6 us (19%)
  local copies, waits for them, and re-layouts  28.8 us (18%)
  starting transfers between devices  11.5 us (7%)
  matrix products  10.1 us (6%)
  waiting for transfers between devices  9.31 us (6%)
    pallas_call x1, Pallas kernels, solve_flow(): pl.pallas_call(functools.partial(flow_kernel, gx_count, sp_count, inner),...  32.6 us
    unnamed x47, local copies, waits for them, and re-layouts  18.1 us
    mul x2, other arithmetic, solve_system(): forward.append(running * inverse[i])  14.5 us
    all_gather x1, blocking collectives, per_device(): lax.all_gather(conduct, 'sp', axis=2, tiled=True)  11.6 us
    all_to_all x1, blocking collectives, per_device(): lax.all_to_all(reacted, 'sp', split_axis=0, concat_axis=3, tiled=True)  9.79 us
    all_gather x1, blocking collectives, per_device(): lax.all_gather(head_field, 'sp', axis=2, tiled=True)  9.2 us
    mul x2, other arithmetic, solve_system(): answer[i] = running * inverse[i]  8.24 us
    dot_general x2, matrix products, reaction(): jnp.dot(pair_products, rate_cells * (1.0 - tangent * tangent), precision=...  7.77 us
  transfers between devices with their start and end apart: 3, of which 2 were waited for; matrix products, arithmetic and copies ran while one was open for 0% of the time, Pallas kernels for 0%

profile of v1, /device:TPU:1, one launch (start us, length us, event | category | flops | bytes accessed | tf_op | source)
XLA Modules:
  0.0 158.6 jit_solution(12664392910377862248)
XLA Ops:
  0.6 0.9 select_reduce_fusion.1
  1.5 11.6 %all_gather.7 = f32[8,8,512]{2,1,0:T(8,128)S(1)} all-gather(f32[8,8,128]{2,1,0:T(8,128)S(1)} %select_reduce_fusion.1), channel_id=1, replica_groups=mesh['gx'=32,'sp'=4] {'sp'}, dimensions={2}, use_global_device_ids=true | all-gather | bytes 163840 | tf_op jit(solution)/shard_map/all_gather | solution.py:487
  13.1 0.8 copy-done
  13.9 0.8 copy-done.1
  14.6 0.8 copy-done.2
  15.4 0.7 copy-done.3
  16.0 0.7 copy-done.4
  16.7 32.6 %shard_map.113 = f32[8,8,128]{2,1,0:T(8,128)S(1)} custom-call(f32[8,8,128]{2,1,0:T(8,128)S(1)} %copy-done.1, f32[8,8,128]{2,1,0:T(8,128)S(1)} %copy-done.2, s32[8,8,128]{2,1,0:T(8,128)S(1)} %copy-done, f32[8]{0:T(128)S(1)} %copy-done.3, f32[8]{0:T(128)S(1)} %copy-done.4), custom_call_target="tpu_custom_call" | custom-call | tf_op jit(solution)/shard_map/pallas_call | solution.py:311
  49.3 9.2 %all_gather.6 = f32[8,8,512]{2,1,0:T(8,128)S(1)} all-gather(f32[8,8,128]{2,1,0:T(8,128)S(1)} %shard_map.113), channel_id=1, replica_groups=mesh['gx'=32,'sp'=4] {'sp'}, dimensions={2}, use_global_device_ids=true | all-gather | bytes 163840 | tf_op jit(solution)/shard_map/all_gather | solution.py:486
  58.5 1.2 copy_dynamic-update-slice_fusion
  59.7 0.1 copy_dynamic-update-slice_fusion.2
  59.9 5.9 %collective-permute-start = (f32[5,8,1,512]{3,1,2,0:T(8,128)S(1)}, f32[5,8,1,512]{3,1,2,0:T(8,128)S(1)}, u32[]{:S(2)}, u32[]{:S(2)}) collective-permute-start(f32[5,8,1,512]{3,1,2,0:T(8,128)S(1)} %get-tuple-element.198), channel_id=1, source_target_pairs={{0,4},{4,8},{8,12},{12,16},{16,20},{20,24},{24,28},{28,32},{32,36}... | collective-permute-start | bytes 245768 | tf_op jit(solution)/shard_map/ppermute | solution.py:344
  65.9 1.9 %collective-permute-start.1 = (f32[5,8,1,512]{3,1,2,0:T(8,128)S(1)}, f32[5,8,1,512]{3,1,2,0:T(8,128)S(1)}, u32[]{:S(2)}, u32[]{:S(2)}) collective-permute-start(f32[5,8,1,512]{3,1,2,0:T(8,128)S(1)} %get-tuple-element.199), channel_id=1, source_target_pairs={{4,0},{8,4},{12,8},{16,12},{20,16},{24,20},{28,24},{32,28},{36,32}... | collective-permute-start | bytes 245768 | tf_op jit(solution)/shard_map/ppermute | solution.py:346
  67.9 3.8 %collective-permute-done.1 = f32[5,8,1,512]{3,1,2,0:T(8,128)S(1)} collective-permute-done((f32[5,8,1,512]{3,1,2,0:T(8,128)S(1)}, f32[5,8,1,512]{3,1,2,0:T(8,128)S(1)}, u32[]{:S(2)}, u32[]{:S(2)}) %collective-permute-start.1) | collective-permute-done | bytes 81952 | tf_op jit(solution)/shard_map/ppermute | solution.py:346
  71.6 0.7 select_maximum_fusion
  72.4 0.2 broadcast_multiply_fusion.5
  72.6 0.3 broadcast_maximum_fusion.4
  73.0 0.3 broadcast_maximum_fusion.5
  73.3 0.4 broadcast_minimum_fusion.5
  73.7 0.2 copy-done.5
  74.0 1.0 multiply_subtract_fusion.2
  74.9 4.1 %copy.52 = f32[3,8,8,512]{2,1,0,3:T(8,128)} copy(f32[3,8,8,512]{3,1,2,0:T(8,128)S(1)} %multiply_subtract_fusion.2) | data formatting | bytes 786432 | tf_op jit(solution)/shard_map/sub | solution.py:393
  79.1 6.1 %reshape.92 = f32[4,1,24576]{2,1,0:T(1,128)} reshape(f32[512,3,8,8]{3,2,1,0:T(8,128)} %bitcast.69) | data formatting | bytes 786432
  85.1 3.6 %all-to-all-start = ((f32[4,1,24576]{2,1,0:T(1,128)}), f32[4,1,24576]{2,1,0:T(1,128)S(1)}, u32[]{:S(2)}, u32[]{:S(2)}) async-start(f32[4,1,24576]{2,1,0:T(1,128)} %reshape.92), calls=%async_computation | async-start | bytes 786432 | tf_op jit(solution)/shard_map/all_to_all | solution.py:467
  88.9 0.1 mul.14434
  89.0 0.3 select_reduce_fusion
  89.3 5.5 %all-to-all-done = f32[4,1,24576]{2,1,0:T(1,128)S(1)} async-done(((f32[4,1,24576]{2,1,0:T(1,128)}), f32[4,1,24576]{2,1,0:T(1,128)S(1)}, u32[]{:S(2)}, u32[]{:S(2)}) %all-to-all-start) | async-done | bytes 393248 | tf_op jit(solution)/shard_map/all_to_all | solution.py:467
  94.8 0.5 broadcast.1007
  95.3 1.8 %reduce = f32[4,24576]{1,0:T(4,128)S(1)} reduce(f32[4,1,24576]{2,1,0:T(1,128)S(1)} %all-to-all-done, f32[]{:T(128)} %broadcast.1007), dimensions={1}, to_apply=%all_to_all.24.reduce_sub_computation | reduce | bytes 786436 | tf_op jit(solution)/shard_map/all_to_all | solution.py:467
  97.1 6.2 %reshape.93 = f32[512,3,8,8]{3,2,1,0:T(8,128)} reshape(f32[4,24576]{1,0:T(4,128)S(1)} %reduce) | data formatting | bytes 786432
  103.3 4.3 %copy.53 = f32[3,8,8,4,128]{4,2,1,0,3:T(8,128)S(1)} copy(f32[3,8,8,4,128]{2,1,0,4,3:T(8,128)} %bitcast.70) | data formatting | bytes 786432 | tf_op jit(solution)/shard_map/all_to_all | solution.py:467
  107.7 0.4 fusion.7
  108.2 0.7 fusion.3
  108.8 3.9 %convolution_multiply_fusion.1 = f32[144,8192]{1,0:T(8,128)S(1)} fusion(f32[144,8]{0,1:T(8,128)S(1)} %mul.14434, f32[8,8192]{1,0:T(8,128)S(1)} %select_reduce_fusion, f32[8,8192]{1,0:T(8,128)S(1)} %fusion.7), kind=kOutput, calls=%fused_computation.1 | convolution fusion | flops 114622464 | bytes 5247488 | tf_op jit(solution)/shard_map/dot_general | solution.py:452
  112.7 7.2 %subtract_multiply_fusion.64 = (f32[1,8192]{1,0:T(1,128)S(1)}, f32[1,8192]{1,0:T(1,128)S(1)}, f32[1,8192]{1,0:T(1,128)S(1)}, f32[1,8192]{1,0:T(1,128)S(1)}, f32[...) fusion(f32[12,8192]{1,0:T(8,128)S(1)} %fusion.3, ...), kind=kLoop, calls=%fused_computation.651 | loop fusion | flops 5136384 | bytes 4751360 | tf_op jit(solution)/shard_map/mul | solution.py:416
  120.0 3.0 %subtract_multiply_fusion.57 = (f32[1,8192]{1,0:T(1,128)S(1)}, f32[1,8192]{1,0:T(1,128)S(1)}, f32[1,8192]{1,0:T(1,128)S(1)}, f32[1,8192]{1,0:T(1,128)S(1)}, f32[...) fusion(f32[1,8192]{1,0:T(1,128)S(1)} %get-tuple-element.116, ...), kind=kLoop, calls=%fused_computation.643 | loop fusion | flops 1654784 | bytes 2883584 | tf_op jit(solution)/shard_map/mul | solution.py:410
  123.0 4.1 %subtract_multiply_fusion.46 = (f32[1,8192]{1,0:T(1,128)S(1)}, f32[1,8192]{1,0:T(1,128)S(1)}, f32[1,8192]{1,0:T(1,128)S(1)}, f32[1,8192]{1,0:T(1,128)S(1)}, f32[...) fusion(f32[1,8192]{1,0:T(1,128)S(1)} %get-tuple-element.183, ...), kind=kLoop, calls=%fused_computation.632 | loop fusion | flops 2220032 | bytes 3342336 | tf_op jit(solution)/shard_map/mul | solution.py:422
  127.1 0.6 stack.93
  127.7 0.5 fusion.5
  128.2 0.7 fusion.1
  128.9 3.9 %convolution_multiply_fusion = f32[144,8192]{1,0:T(8,128)S(1)} fusion(f32[144,8]{0,1:T(8,128)S(1)} %mul.14434, f32[8,8192]{1,0:T(8,128)S(1)} %select_reduce_fusion, f32[8,8192]{1,0:T(8,128)S(1)} %fusion.5), kind=kOutput, calls=%fused_computation | convolution fusion | flops 114622464 | bytes 5247488 | tf_op jit(solution)/shard_map/dot_general | solution.py:452
  132.8 7.3 %subtract_multiply_fusion.18 = (f32[1,8192]{1,0:T(1,128)S(1)}, f32[1,8192]{1,0:T(1,128)S(1)}, f32[1,8192]{1,0:T(1,128)S(1)}, f32[1,8192]{1,0:T(1,128)S(1)}, f32[...) fusion(f32[12,8192]{1,0:T(8,128)S(1)} %fusion.1, ...), kind=kLoop, calls=%fused_computation.597 | loop fusion | flops 5136384 | bytes 4751360 | tf_op jit(solution)/shard_map/mul | solution.py:416
  140.1 2.7 %subtract_multiply_fusion.11 = (f32[1,8192]{1,0:T(1,128)S(1)}, f32[1,8192]{1,0:T(1,128)S(1)}, f32[1,8192]{1,0:T(1,128)S(1)}, f32[1,8192]{1,0:T(1,128)S(1)}, f32[...) fusion(f32[1,8192]{1,0:T(1,128)S(1)} %get-tuple-element.25, ...), kind=kLoop, calls=%fused_computation.589 | loop fusion | flops 1654784 | bytes 2883584 | tf_op jit(solution)/shard_map/mul | solution.py:410
  142.9 4.1 %subtract_multiply_fusion = (f32[1,8192]{1,0:T(1,128)S(1)}, f32[1,8192]{1,0:T(1,128)S(1)}, f32[1,8192]{1,0:T(1,128)S(1)}, f32[1,8192]{1,0:T(1,128)S(1)}, f32[1,8...) fusion(f32[1,8192]{1,0:T(1,128)S(1)} %get-tuple-element.92, ...), kind=kLoop, calls=%fused_computation.578 | loop fusion | flops 2220032 | bytes 3342336 | tf_op jit(solution)/shard_map/mul | solution.py:422
  147.3 0.1 fusion.11
  147.4 9.8 %all_to_all.33 = f32[12,8,8,128]{3,2,1,0:T(8,128)S(1)} all-to-all(f32[12,8,8,128]{3,2,1,0:T(8,128)S(1)} %fusion.11), channel_id=1, replica_groups=mesh['gx'=32,'sp'=4] {'sp'}, dimensions={0} | all-to-all | bytes 786432 | tf_op jit(solution)/shard_map/all_to_all | solution.py:499
  157.2 0.8 copy.60
  158.0 0.6 copy.86
  (44 shorter events, 0.5 us)
Async XLA Ops:
  0.6 67.2 %copy-start.7 = (s32[8,8,128]{2,1,0:T(8,128)S(1)}, s32[8,8,128]{2,1,0:T(8,128)}, u32[]{:S(2)}) copy-start(s32[8,8,128]{2,1,0:T(8,128)} %param.16) | copy-start | bytes 98308
  13.1 0.8 copy-start
  13.9 0.8 copy-start.1
  14.6 0.8 copy-start.2
  15.4 0.7 copy-start.3
  16.0 0.7 copy-start.4
  59.9 7.9 %collective-permute-start = (f32[5,8,1,512]{3,1,2,0:T(8,128)S(1)}, f32[5,8,1,512]{3,1,2,0:T(8,128)S(1)}, u32[]{:S(2)}, u32[]{:S(2)}) collective-permute-start(f32[5,8,1,512]{3,1,2,0:T(8,128)S(1)} %get-tuple-element.198), channel_id=1, source_target_pairs={{0,4},{4,8},{8,12},{12,16},{16,20},{20,24},{24,28},{28,32},{32,36}... | collective-permute-start | bytes 245768 | tf_op jit(solution)/shard_map/ppermute | solution.py:344
  65.9 5.8 %collective-permute-start.1 = (f32[5,8,1,512]{3,1,2,0:T(8,128)S(1)}, f32[5,8,1,512]{3,1,2,0:T(8,128)S(1)}, u32[]{:S(2)}, u32[]{:S(2)}) collective-permute-start(f32[5,8,1,512]{3,1,2,0:T(8,128)S(1)} %get-tuple-element.199), channel_id=1, source_target_pairs={{4,0},{8,4},{12,8},{16,12},{20,16},{24,20},{28,24},{32,28},{36,32}... | collective-permute-start | bytes 245768 | tf_op jit(solution)/shard_map/ppermute | solution.py:346
  73.0 1.0 copy-start.5
  79.1 9.7 %copy-start.6 = (f32[12,8]{0,1:T(8,128)S(1)}, f32[12,8]{0,1:T(8,128)}, u32[]{:S(2)}) copy-start(f32[12,8]{0,1:T(8,128)} %param.18) | copy-start | bytes 1156
  79.1 9.9 %copy-start.8 = (f32[6,8]{1,0:T(8,128)S(1)}, f32[6,8]{1,0:T(8,128)}, u32[]{:S(2)}) copy-start(f32[6,8]{1,0:T(8,128)} %param.17) | copy-start | bytes 580
  85.1 9.7 %all-to-all-start = ((f32[4,1,24576]{2,1,0:T(1,128)}), f32[4,1,24576]{2,1,0:T(1,128)S(1)}, u32[]{:S(2)}, u32[]{:S(2)}) async-start(f32[4,1,24576]{2,1,0:T(1,128)} %reshape.92), calls=%async_computation | async-start | bytes 786432 | tf_op jit(solution)/shard_map/all_to_all | solution.py:467
  103.3 4.4 %copy-start.9 = (f32[8]{0:T(128)S(1)}, f32[8]{0:T(128)}, u32[]{:S(2)}) copy-start(f32[8]{0:T(128)} %param.19) | copy-start | bytes 100

commit v2 on v1

v2 whole, which is shorter than its diff:
```python
import functools

import jax
import jax.numpy as jnp
from jax import lax
from jax.experimental import pallas as pl
from jax.experimental.pallas import tpu as pltpu
from jax.sharding import PartitionSpec as P

NEWTON = 2
BLOCK = 3

time_step = 0.05
dispersion = 0.5
reaction_span = 0.5
newton_damping = 0.5

MESH = pl.DeviceIdType.MESH
EXACT = lax.Precision.HIGHEST


def table_lookup(labels, table):
    size = table.shape[0] if hasattr(table, "shape") else len(table)
    found = jnp.full(labels.shape, table[0], jnp.float32)
    for level in range(1, size):
        found = jnp.where(labels == level, table[level], found)
    return found


def harmonic_safe(center, other):
    return 2.0 * center * other / jnp.maximum(center + other, 1e-30)


def shifted(field, offset, axis):
    size = field.shape[axis]
    return pltpu.roll(field, (-offset) % size, axis)


def layer_above(field):
    return jnp.concatenate([field[1:], field[-1:]], axis=0)


def layer_below(field):
    return jnp.concatenate([field[:1], field[:-1]], axis=0)


def six_faces(conduct):
    east = harmonic_safe(conduct, shifted(conduct, 1, 2))
    south = harmonic_safe(conduct, shifted(conduct, 1, 1))
    top = harmonic_safe(conduct[:-1], conduct[1:])
    none = jnp.zeros_like(conduct[:1])
    return (
        jnp.concatenate([top, none], axis=0),
        jnp.concatenate([none, top], axis=0),
        south,
        shifted(south, -1, 1),
        east,
        shifted(east, -1, 2),
    )


def six_beside(field):
    return (
        layer_above(field),
        layer_below(field),
        shifted(field, 1, 1),
        shifted(field, -1, 1),
        shifted(field, 1, 2),
        shifted(field, -1, 2),
    )


def apply_flow(field, storage, faces):
    result = storage * field
    for face, beside in zip(faces, six_beside(field)):
        result = result + face * (field - beside)
    return result


def add_scaled(left, scale, right):
    total = dict(left)
    for key, value in right.items():
        term = scale * value
        total[key] = total[key] + term if key in total else term
    return total


def cg_block(rr, pr, pp, least, most, same):
    one = jnp.ones_like(least)
    direction = {(0, 0): one}
    residual = {(0 if same else 1, 0): one}
    change = {}
    live = None
    for step in range(BLOCK):
        alpha = (pr if step == 0 else rr)[0] / jnp.maximum(pp[1], 1e-30)
        alpha = jnp.clip(alpha, least, most)
        if live is not None:
            alpha = jnp.where(live, alpha, 0.0)
        change = add_scaled(change, alpha, direction)
        image = {(part, power + 1): value for (part, power), value in direction.items()}
        residual = add_scaled(residual, -alpha, image)
        if len(pp) < 3 or len(pr) < 2:
            break
        square = alpha * alpha
        count = min(len(rr), len(pr) - 1, len(pp) - 2)
        next_rr = [rr[k] - 2.0 * alpha * pr[k + 1] + square * pp[k + 2] for k in range(count)]
        count = min(len(pr), len(pp) - 1)
        next_pr = [pr[k] - alpha * pp[k + 1] for k in range(count)]
        above = next_rr[0] > 1e-6 * (rr[0] + square * pp[2])
        live = above if live is None else live & above
        beta = jnp.where(live, next_rr[0] / jnp.maximum(rr[0], 1e-37), 0.0)
        direction = add_scaled(residual, beta, direction)
        count = min(len(next_rr), len(next_pr))
        next_pp = [
            next_rr[k] + 2.0 * beta * next_pr[k] + beta * beta * pp[k] for k in range(count)
        ]
        pr = [next_rr[k] + beta * next_pr[k] for k in range(count)]
        rr, pp = next_rr, next_pp
    return change, residual, direction


def combine(polynomial, parts):
    total = None
    for (part, power), value in sorted(polynomial.items()):
        term = value[None] * parts[part][power]
        total = term if total is None else total + term
    return total


def column_edges(pick, block):
    return lax.dot_general(
        pick,
        block,
        (((1,), (1,)), ((), ())),
        precision=EXACT,
        preferred_element_type=jnp.float32,
    )


def spread_edges(edges, pick):
    return lax.dot_general(
        edges,
        pick,
        (((0,), (0,)), ((), ())),
        precision=EXACT,
        preferred_element_type=jnp.float32,
    )


def weighted(scales, fields):
    total = None
    for scale, field in zip(scales, fields):
        term = scale * field
        total = term if total is None else total + term
    return total


def mineral_correction(gram, slope, start):
    count = len(start)
    right = [weighted([gram[i][k] for k in range(count)], start) for i in range(count)]
    schur = {(i, j): gram[i][j] for i in range(count) for j in range(i + 1)}
    pivot, lower = [None] * count, {}
    for k in range(count):
        pivot[k] = slope[k] / (1.0 + slope[k] * schur[k, k])
        for i in range(k + 1, count):
            lower[i, k] = schur[i, k] * pivot[k]
        for i in range(k + 1, count):
            right[i] = right[i] - lower[i, k] * right[k]
            for j in range(k + 1, i + 1):
                schur[i, j] = schur[i, j] - lower[i, k] * schur[j, k]
    answer = [None] * count
    for k in reversed(range(count)):
        value = pivot[k] * right[k]
        for i in range(k + 1, count):
            value = value - lower[i, k] * answer[i]
        answer[k] = value
    return answer


def react(moved, labels, rate_table, stoich, log_equil, gram):
    zones, minerals = rate_table.shape
    species = len(moved)
    rates = [table_lookup(labels, [rate_table[z, m] for z in range(zones)]) for m in range(minerals)]
    base = [
        weighted([stoich[c, m] for c in range(species)], moved) - log_equil[m]
        for m in range(minerals)
    ]
    extent = None
    for newton_pass in range(NEWTON):
        affinity = base
        if extent is not None:
            affinity = [base[m] + weighted(gram[m], extent) for m in range(minerals)]
        tangent = [jnp.tanh(value) for value in affinity]
        start = [reaction_span * rates[m] * tangent[m] for m in range(minerals)]
        if extent is not None:
            start = [extent[m] + start[m] for m in range(minerals)]
        slope = [
            reaction_span * rates[m] * jnp.maximum(1.0 - tangent[m] * tangent[m], 0.0)
            for m in range(minerals)
        ]
        correction = mineral_correction(gram, slope, start)
        step = [newton_damping * (start[m] - correction[m]) for m in range(minerals)]
        extent = [-step[m] if extent is None else extent[m] - step[m] for m in range(minerals)]
    return [
        moved[c] + weighted([stoich[c, m] for m in range(minerals)], extent)
        for c in range(species)
    ]


def step_kernel(
    gx_count,
    sp_count,
    inner,
    previous_head_in,
    recharge_in,
    soil_zone_in,
    soil_cond,
    soil_store,
    species_in,
    mineral_zone_in,
    rate_table,
    stoich,
    log_equil,
    head_out,
    species_out,
    previous_head,
    recharge,
    soil_zone,
    mineral_zone,
    species,
    field,
    rows_in,
    edge_out,
    edge_in,
    near_0,
    far_0,
    near_1,
    far_1,
    conc,
    ends_out,
    ends_in,
    sides_out,
    sides_in,
    beside_conc,
    weights,
    moved,
    reacted,
    gram_table,
    load_sem,
    halo_send,
    halo_recv,
    sum_send,
    sum_recv,
    spread_send,
    spread_recv,
    result_sem,
):
    g = lax.axis_index("gx")
    s = lax.axis_index("sp")
    outer = gx_count // inner
    low, high = g % inner, g // inner
    plane = high * sp_count + s
    near_peers = [(high * inner + (low + k) % inner, s) for k in range(1, inner)]
    far_peers = [
        (((high + k // sp_count) % outer) * inner + low, (s + k % sp_count) % sp_count)
        for k in range(1, outer * sp_count)
    ]
    group = species_in.shape[0]
    layers = species_in.shape[1]

    def columns_of(device):
        return pl.ds(pl.multiple_of(device * 128, 128), 128)

    def beside(rows, columns):
        return ((g + rows + gx_count) % gx_count, (s + columns) % sp_count)

    def remote(source, target, send, recv, peer):
        copy = pltpu.make_async_remote_copy(
            src_ref=source,
            dst_ref=target,
            send_sem=send,
            recv_sem=recv,
            device_id=peer,
            device_id_type=MESH,
        )
        copy.start()
        return copy

    loads = [
        pltpu.make_async_copy(source, target, load_sem.at[number])
        for number, (source, target) in enumerate(
            (
                (soil_zone_in, soil_zone),
                (previous_head_in, previous_head),
                (recharge_in, recharge),
                (species_in, species),
                (species_in.at[:, :, :, columns_of(s)], conc.at[pl.ds(group * s, group)]),
                (mineral_zone_in, mineral_zone),
            )
        )
    ]
    for copy in loads:
        copy.start()

    offsets = [(rows, columns) for rows in (-1, 0, 1) for columns in (-1, 0, 1) if (rows, columns) != (0, 0)]
    others = [k for k in range(2, sp_count - 1)]
    barrier = pltpu.get_barrier_semaphore()
    peers = [beside(*offset) for offset in offsets] + near_peers + far_peers
    peers += [beside(rows, k) for rows in (-1, 1) for k in others]
    for peer in peers:
        pl.semaphore_signal(barrier, inc=1, device_id=peer, device_id_type=MESH)

    for copy in loads[:3]:
        copy.wait()
    zone = soil_zone[...]
    field[0] = table_lookup(zone, soil_store) * previous_head[...] + recharge[...]
    field[1] = zone.astype(jnp.float32)
    line = lax.broadcasted_iota(jnp.int32, (16, 128), 0)
    lane = lax.broadcasted_iota(jnp.int32, (16, 128), 1)
    pick = (lane == jnp.where(line < 8, line, line + 112)).astype(jnp.float32)
    edge_out[...] = column_edges(pick, field[...].reshape(128, 128))

    pl.semaphore_wait(barrier, len(peers))
    halo = []
    for number, (rows, columns) in enumerate(offsets):
        if columns == 0:
            source, target = field, rows_in.at[0 if rows == 1 else 1]
        else:
            first = 8 if columns == 1 else 0
            source = edge_out.at[pl.ds(first, 8)]
            target = edge_in.at[1 - rows, pl.ds(first, 8)]
        halo.append(
            remote(source, target, halo_send.at[number], halo_recv.at[number], beside(rows, columns))
        )

    mine = pl.ds(group * s, group)
    loads[3].wait()
    for k in range(1, sp_count):
        to = (s + k) % sp_count
        remote(
            species.at[:, :, :, columns_of(to)],
            conc.at[mine],
            spread_send.at[0],
            spread_recv.at[0],
            (g, to),
        )
    width = species.shape[3]
    line = lax.broadcasted_iota(jnp.int32, (2 * sp_count, width), 0)
    lane = lax.broadcasted_iota(jnp.int32, (2 * sp_count, width), 1)
    wanted = jnp.where(line % 2 == 0, (line // 2) * 128 - 1, (line // 2) * 128 + 128)
    tiles = group * layers * 8
    sides_out[:, :tiles] = column_edges(
        (lane == wanted).astype(jnp.float32), species[...].reshape(tiles, width)
    )
    for layer in range(layers):
        ends_out[0, :, layer : layer + 1, :] = species[:, layer, 0:1, :]
        ends_out[1, :, layer : layer + 1, :] = species[:, layer, 7:8, :]
    sides_in[s] = sides_out[...]
    for k in range(1, sp_count):
        to = (s + k) % sp_count
        remote(sides_out, sides_in.at[s], spread_send.at[1], spread_recv.at[1], (g, to))
    for k in range(sp_count):
        to = (s + k) % sp_count
        for rows in (-1, 1):
            remote(
                ends_out.at[0 if rows == -1 else 1, :, :, columns_of(to)],
                ends_in.at[1 if rows == -1 else 0, mine],
                spread_send.at[2],
                spread_recv.at[2],
                beside(rows, k),
            )

    for copy in halo:
        copy.wait_recv()

    row_blocks = []
    for block, center in enumerate((rows_in[0], field[...], rows_in[1])):
        side = spread_edges(edge_in[block], pick).reshape(2, 8, 8, 128)
        row_blocks.append(jnp.concatenate([center, side], axis=3))
    wide = jnp.concatenate(row_blocks, axis=2)
    row = lax.broadcasted_iota(jnp.int32, (24, 256), 0)
    column = lax.broadcasted_iota(jnp.int32, (24, 256), 1)
    first_row = jnp.where(g > 0, 0, 8)
    end_row = jnp.where(g < gx_count - 1, 24, 16)
    end_right = jnp.where(s < sp_count - 1, 136, 128)
    first_left = jnp.where(s > 0, 248, 256)
    inside = (
        (row >= first_row)
        & (row < end_row)
        & ((column < end_right) | (column >= first_left))
    )[None]
    source = jnp.where(inside, wide[0], 0.0)
    conduct = jnp.where(inside, table_lookup(wide[1], soil_cond), 0.0)
    storage = jnp.where(inside, table_lookup(wide[1], soil_store), 0.0)
    faces = six_faces(conduct)

    store_least, store_most, cond_most = soil_store[0], soil_store[0], soil_cond[0]
    for level in range(1, soil_store.shape[0]):
        store_least = jnp.minimum(store_least, soil_store[level])
        store_most = jnp.maximum(store_most, soil_store[level])
        cond_most = jnp.maximum(cond_most, soil_cond[level])
    most = 1.0 / jnp.full((1, 256), store_least, jnp.float32)
    least = 1.0 / jnp.full((1, 256), store_most + 12.0 * cond_most, jnp.float32)

    sends = []

    def exchange(buffer, slot, value, to_peers, number, meanwhile):
        buffer[slot] = value
        for peer in to_peers:
            remote(buffer.at[slot], buffer.at[slot], sum_send.at[number], sum_recv.at[number], peer)
        if meanwhile is not None:
            meanwhile()
        all_others = buffer.at[pl.ds(0, len(to_peers))]
        pltpu.make_async_copy(all_others, all_others, sum_recv.at[number]).wait()
        sends.append(pltpu.make_async_copy(all_others, all_others, sum_send.at[number]))
        return jnp.sum(buffer[...], axis=0)

    def global_sums(pairs, near, far, number, first_work, second_work):
        lines = near.shape[1]
        index = lax.broadcasted_iota(jnp.int32, (lines, 128), 0)
        partial = jnp.zeros((lines, 128), jnp.float32)
        for position, (left, right) in enumerate(pairs):
            product = left[:, 8:16, :128] * right[:, 8:16, :128]
            total = jnp.sum(jnp.sum(product, axis=0), axis=0, keepdims=True)
            partial = jnp.where(index == position, total, partial)
        partial = exchange(near, low, partial, near_peers, number, first_work)
        partial = exchange(far, plane, partial, far_peers, number + 1, second_work)
        totals = jnp.broadcast_to(jnp.sum(partial, axis=1, keepdims=True), (lines, 256))
        return [totals[k : k + 1] for k in range(len(pairs))]

    species_count, mineral_count = stoich.shape

    def fill_gram():
        columns = [
            [stoich[c, m] for c in range(species_count)] for m in range(mineral_count)
        ]
        for i in range(mineral_count):
            for j in range(i + 1):
                terms = [a * b for a, b in zip(columns[i], columns[j])]
                while len(terms) > 1:
                    terms = [sum(terms[k : k + 2][1:], terms[k]) for k in range(0, len(terms), 2)]
                gram_table[i, j] = terms[0]

    def place_species():
        whole = conc.at[pl.ds(0, group * (sp_count - 1))]
        pltpu.make_async_copy(whole, whole, spread_recv.at[0]).wait()
        part = sides_in.at[pl.ds(0, sp_count - 1)]
        pltpu.make_async_copy(part, part, spread_recv.at[1]).wait()
        pltpu.make_async_copy(ends_in, ends_in, spread_recv.at[2]).wait()
        loads[4].wait()
        line = lax.broadcasted_iota(jnp.int32, (2 * sp_count, 128), 0)
        lane = lax.broadcasted_iota(jnp.int32, (2 * sp_count, 128), 1)
        place = (((line == 2 * s) & (lane == 0)) | ((line == 2 * s + 1) & (lane == 127))).astype(
            jnp.float32
        )
        row = lax.broadcasted_iota(jnp.int32, (1, 1, 8, 128), 2)
        lane = lax.broadcasted_iota(jnp.int32, (1, 1, 8, 128), 3)
        shape = (group, layers, 8, 128)
        for block in range(sp_count):
            part = pl.ds(group * block, group)
            center = conc[part]
            edges = spread_edges(sides_in[block][:, :tiles], place).reshape(shape)
            upper = jnp.broadcast_to(ends_in[0, part][:, :, None, :], shape)
            under = jnp.broadcast_to(ends_in[1, part][:, :, None, :], shape)
            beside_conc[0, part] = jnp.where(row == 7, under, shifted(center, 1, 2))
            beside_conc[1, part] = jnp.where(row == 0, upper, shifted(center, -1, 2))
            beside_conc[2, part] = jnp.where(lane == 127, edges, shifted(center, 1, 3))
            beside_conc[3, part] = jnp.where(lane == 0, edges, shifted(center, -1, 3))

    powers = [source]
    for k in range(BLOCK):
        powers.append(apply_flow(powers[-1], storage, faces))
    pairs = [(powers[k // 2], powers[(k + 1) // 2]) for k in range(2 * BLOCK + 1)]
    moments = global_sums(pairs, near_0, far_0, 0, fill_gram, None)
    change, residual, direction = cg_block(moments, moments, moments, least, most, True)
    head = combine(change, [powers])
    residual = combine(residual, [powers])
    direction = combine(direction, [powers])

    p_powers = [direction]
    for k in range(BLOCK):
        p_powers.append(apply_flow(p_powers[-1], storage, faces))
    r_powers = [residual]
    for k in range(BLOCK - 1):
        r_powers.append(apply_flow(r_powers[-1], storage, faces))
    pairs = [(r_powers[k // 2], r_powers[(k + 1) // 2]) for k in range(4)]
    pairs += [(p_powers[(k + 1) // 2], r_powers[k // 2]) for k in range(5)]
    pairs += [(p_powers[k // 2], p_powers[(k + 1) // 2]) for k in range(6)]
    moments = global_sums(pairs, near_1, far_1, 2, place_species, None)
    change, _, _ = cg_block(moments[:4], moments[4:9], moments[9:], least, most, False)
    head = head + combine(change, [p_powers, r_powers])

    def own(values):
        return values[:, 8:16, :128]

    head_out[...] = own(head)
    kept = jnp.ones_like(own(head))
    for number, (face, head_beside) in enumerate(zip(faces, six_beside(head))):
        face = own(face)
        velocity = face * (own(head) - own(head_beside))
        kept = kept - time_step * (jnp.maximum(velocity, 0.0) + dispersion * face)
        weights[number] = time_step * (dispersion * face - jnp.minimum(velocity, 0.0))
    for number in range(species_count):
        center = conc[number]
        total = kept * center
        total = total + weights[0] * layer_above(center)
        total = total + weights[1] * layer_below(center)
        for side in range(4):
            total = total + weights[2 + side] * beside_conc[side, number]
        moved[number] = total

    loads[5].wait()
    chunk = 2

    def react_chunk(step, carry):
        span = pl.ds(step * chunk, chunk)
        gram = [
            [gram_table[max(i, j), min(i, j)] for j in range(mineral_count)]
            for i in range(mineral_count)
        ]
        result = react(
            [moved[c, span] for c in range(species_count)],
            mineral_zone[span],
            rate_table,
            stoich,
            log_equil,
            gram,
        )
        for c in range(species_count):
            reacted[c, span] = result[c]
        for k in range(1, sp_count):
            to = (s + k) % sp_count
            remote(
                reacted.at[pl.ds(group * to, group), span],
                species_out.at[:, span, :, columns_of(s)],
                result_sem.at[0],
                result_sem.at[1],
                (g, to),
            )
        pltpu.make_async_copy(
            reacted.at[mine, span], species_out.at[:, span, :, columns_of(s)], result_sem.at[2]
        ).start()
        return carry

    lax.fori_loop(0, layers // chunk, react_chunk, 0)

    for copy in halo:
        copy.wait_send()
    for copy in sends:
        copy.wait()
    three = conc.at[pl.ds(0, group * (sp_count - 1))]
    pltpu.make_async_copy(three, three, spread_send.at[0]).wait()
    part = sides_in.at[pl.ds(0, sp_count - 1)]
    pltpu.make_async_copy(part, part, spread_send.at[1]).wait()
    pltpu.make_async_copy(ends_in, ends_in, spread_send.at[2]).wait()
    pltpu.make_async_copy(three, three, result_sem.at[0]).wait()
    pltpu.make_async_copy(three, three, result_sem.at[1]).wait()
    once = reacted.at[pl.ds(0, group)]
    pltpu.make_async_copy(once, once, result_sem.at[2]).wait()


def per_device(mesh, *arrays):
    gx_count, sp_count = mesh.shape["gx"], mesh.shape["sp"]
    inner = min(8, gx_count // 2)
    far_count = gx_count // inner * sp_count
    species = arrays[5]
    group, layers, _, width = species.shape
    total = group * sp_count
    minerals = arrays[8].shape[1]
    vmem = pl.BlockSpec(memory_space=pltpu.VMEM)
    smem = pl.BlockSpec(memory_space=pltpu.SMEM)
    hbm = pl.BlockSpec(memory_space=pltpu.HBM)
    cells = (layers, 8, 128)

    def floats(*shape):
        return pltpu.VMEM(shape, jnp.float32)

    return tuple(
        pl.pallas_call(
            functools.partial(step_kernel, gx_count, sp_count, inner),
            out_shape=(
                jax.ShapeDtypeStruct(cells, jnp.float32),
                jax.ShapeDtypeStruct(species.shape, jnp.float32),
            ),
            in_specs=[hbm, hbm, hbm, smem, smem, hbm, hbm, smem, smem, smem],
            out_specs=(vmem, hbm),
            scratch_shapes=[
                floats(*cells),
                floats(*cells),
                pltpu.VMEM(cells, jnp.int32),
                pltpu.VMEM(cells, jnp.int32),
                floats(*species.shape),
                floats(2, *cells),
                floats(2, 2, *cells),
                floats(16, 128),
                floats(3, 16, 128),
                floats(inner, 8, 128),
                floats(far_count, 8, 128),
                floats(inner, 16, 128),
                floats(far_count, 16, 128),
                floats(total, *cells),
                floats(2, group, layers, width),
                floats(2, total, layers, 128),
                floats(2 * sp_count, 256),
                floats(sp_count, 2 * sp_count, 256),
                floats(4, total, *cells),
                floats(6, *cells),
                floats(total, *cells),
                floats(total, *cells),
                pltpu.SMEM((minerals, minerals), jnp.float32),
                pltpu.SemaphoreType.DMA((6,)),
                pltpu.SemaphoreType.DMA((8,)),
                pltpu.SemaphoreType.DMA((8,)),
                pltpu.SemaphoreType.DMA((4,)),
                pltpu.SemaphoreType.DMA((4,)),
                pltpu.SemaphoreType.DMA((3,)),
                pltpu.SemaphoreType.DMA((3,)),
                pltpu.SemaphoreType.DMA((3,)),
            ],
            compiler_params=pltpu.CompilerParams(
                collective_id=0, has_side_effects=True, vmem_limit_bytes=48 * 1024 * 1024
            ),
        )(*arrays)
    )


def solution(mesh):
    cells = P(None, "gx", "sp")
    groups = P("sp", None, "gx", None)
    return jax.shard_map(
        functools.partial(per_device, mesh),
        mesh=mesh,
        in_specs=(cells, cells, cells, P(), P(), groups, cells, P(), P(), P()),
        out_specs=(cells, groups),
        check_vma=False,
    )
```

time: 161 us -> 47.4 us (0.29); the launches traced: 159 us -> 46.9 us
  other arithmetic: 34.6 us -> 0 us
  blocking collectives: 30.6 us -> 0 us
  local copies, waits for them, and re-layouts: 28.8 us -> 6.19 us
  starting transfers between devices: 11.5 us -> 0 us
  matrix products: 10.1 us -> 0 us
  waiting for transfers between devices: 9.31 us -> 0 us
  Pallas kernels: 32.6 us -> 40 us
    mul x8 -> x0, other arithmetic: 28.8 us -> none  [the longest x2 14.5 us: solve_system(): forward.append(running * inverse[i])]
    all_gather x2 -> x0, blocking collectives: 20.8 us -> none  [the longest x1 11.6 us: per_device(): lax.all_gather(conduct, 'sp', axis=2, tiled=True)]
    unnamed x47 -> x21, local copies, waits for them, and re-layouts: 18.1 us -> 6.19 us
    dot_general x6 -> x0, matrix products: 10.1 us -> none  [the longest x2 7.77 us: reaction(): jnp.dot(pair_products, rate_cells * (1.0 - tangent * tangent), precision=...]
    all_to_all x1 -> x0, blocking collectives: 9.79 us -> none  [per_device(): lax.all_to_all(reacted, 'sp', split_axis=0, concat_axis=3, tiled=True)]
    ppermute x2 -> x0, starting transfers between devices: 7.87 us -> none  [the longest x1 5.94 us: padded_2(): lax.ppermute(tail, axis, [(i, (i + 1) % count) for i in range(ends)])]
    pallas_call x1, Pallas kernels: 32.6 us -> 40 us  [per_device(): pl.pallas_call(functools.partial(step_kernel, gx_count, sp_count, inner),...]
    all_to_all x3 -> x0, local copies, waits for them, and re-layouts: 5.65 us -> none  [the longest x2 4.86 us: to_cells(): return lax.all_to_all(block, 'sp', split_axis=3, concat_axis=0, tiled=True)]
  transfers between devices with their start and end apart: 3 -> 0, of which waited for: 2 -> 0; matrix products, arithmetic and copies ran while one was open for 0% -> 0% of each run, Pallas kernels for 0% -> 0%
where the time goes in v2:
time: 47.4 us; the launch traced here: 46.9 us
  Pallas kernels  40 us (84%)
  local copies, waits for them, and re-layouts  6.19 us (13%)
  between operations  0.69 us (1%)
    pallas_call x1, Pallas kernels, per_device(): pl.pallas_call(functools.partial(step_kernel, gx_count, sp_count, inner),...  40 us
    unnamed x21, local copies, waits for them, and re-layouts  6.19 us

profile of v2, /device:TPU:1, one launch (start us, length us, event | category | flops | bytes accessed | tf_op | source)
XLA Modules:
  0.0 46.9 jit_solution(3305846815162984872)
XLA Ops:
  0.6 0.0 copy-start.8
  0.6 0.0 copy-start.5
  0.7 0.0 copy-start.7
  0.7 0.0 copy-start.6
  0.7 0.8 %copy.12.stoich = f32[12,8]{1,0:T(8,128)S(1)} copy(f32[12,8]{0,1:T(8,128)} %param.18) | data formatting | bytes 768 | tf_op args[8]
  1.5 0.0 copy-done.8
  1.5 0.0 copy-done.5
  1.5 0.0 copy-done.7
  1.5 0.0 copy-done.6
  1.5 0.0 copy-start
  1.5 1.0 %copy-done = f32[3,8,8,512]{3,2,1,0:T(8,128)S(1)} copy-done((f32[3,8,8,512]{3,2,1,0:T(8,128)S(1)}, f32[3,8,8,512]{3,2,1,0:T(8,128)}, u32[]{:S(2)}) %copy-start) | copy-done | bytes 393240
  2.5 0.0 copy-start.1
  2.5 0.8 %copy-done.1 = f32[8,8,128]{2,1,0:T(8,128)S(1)} copy-done((f32[8,8,128]{2,1,0:T(8,128)S(1)}, f32[8,8,128]{2,1,0:T(8,128)}, u32[]{:S(2)}) %copy-start.1) | copy-done | bytes 32792
  3.2 0.0 copy-start.2
  3.2 0.8 %copy-done.2 = f32[8,8,128]{2,1,0:T(8,128)S(1)} copy-done((f32[8,8,128]{2,1,0:T(8,128)S(1)}, f32[8,8,128]{2,1,0:T(8,128)}, u32[]{:S(2)}) %copy-start.2) | copy-done | bytes 32792
  4.0 0.0 copy-start.3
  4.0 0.8 %copy-done.3 = s32[8,8,128]{2,1,0:T(8,128)S(1)} copy-done((s32[8,8,128]{2,1,0:T(8,128)S(1)}, s32[8,8,128]{2,1,0:T(8,128)}, u32[]{:S(2)}) %copy-start.3) | copy-done | bytes 32792
  4.8 0.0 copy-start.4
  4.8 0.8 %copy-done.4 = s32[8,8,128]{2,1,0:T(8,128)S(1)} copy-done((s32[8,8,128]{2,1,0:T(8,128)S(1)}, s32[8,8,128]{2,1,0:T(8,128)}, u32[]{:S(2)}) %copy-start.4) | copy-done | bytes 32792
  5.5 40.0 %shard_map.113 = (f32[8,8,128]{2,1,0:T(8,128)S(1)}, f32[3,8,8,512]{3,2,1,0:T(8,128)S(1)}) custom-call(f32[8,8,128]{2,1,0:T(8,128)S(1)} %copy-done.1, f32[8,8,128]{2,1,0:T(8,128)S(1)} %copy-done.2, s32[8,8,128]{2,1,0:T(8,128)S(1)} %copy-done.3, f32[8]{0:T(128)S(1)} %copy-done.6, f32[8]{0:T(128)S(1)} %copy-done.7, f32[3,8,8,512]{3,2,1,0:T(8,128)S(1)} %copy-done, ...), custom_call_target="tpu_custom_call" | custom-call | tf_op jit(solution)/shard_map/pallas_call | solution.py:579
  45.5 0.6 %copy.15 = f32[8,8,128]{2,1,0:T(8,128)} copy(f32[8,8,128]{2,1,0:T(8,128)S(1)} %get-tuple-element.4) | data formatting | bytes 65536
  46.2 0.7 %copy.16 = f32[3,8,8,512]{3,2,1,0:T(8,128)} copy(f32[3,8,8,512]{3,2,1,0:T(8,128)S(1)} %get-tuple-element.5) | data formatting | bytes 786432
Async XLA Ops:
  0.6 0.8 %copy-start.8 = (f32[8]{0:T(128)S(1)}, f32[8]{0:T(128)}, u32[]{:S(2)}) copy-start(f32[8]{0:T(128)} %log_equil.1) | copy-start | bytes 100
  0.6 0.8 %copy-start.5 = (f32[6,8]{1,0:T(8,128)S(1)}, f32[6,8]{1,0:T(8,128)}, u32[]{:S(2)}) copy-start(f32[6,8]{1,0:T(8,128)} %rate_table.1) | copy-start | bytes 580
  0.7 0.8 %copy-start.7 = (f32[8]{0:T(128)S(1)}, f32[8]{0:T(128)}, u32[]{:S(2)}) copy-start(f32[8]{0:T(128)} %soil_store.1) | copy-start | bytes 100
  0.7 0.8 %copy-start.6 = (f32[8]{0:T(128)S(1)}, f32[8]{0:T(128)}, u32[]{:S(2)}) copy-start(f32[8]{0:T(128)} %soil_cond.1) | copy-start | bytes 100
  1.5 1.0 %copy-start = (f32[3,8,8,512]{3,2,1,0:T(8,128)S(1)}, f32[3,8,8,512]{3,2,1,0:T(8,128)}, u32[]{:S(2)}) copy-start(f32[3,8,8,512]{3,2,1,0:T(8,128)} %species_in.1) | copy-start | bytes 1179652
  2.5 0.8 %copy-start.1 = (f32[8,8,128]{2,1,0:T(8,128)S(1)}, f32[8,8,128]{2,1,0:T(8,128)}, u32[]{:S(2)}) copy-start(f32[8,8,128]{2,1,0:T(8,128)} %previous_head_in.1) | copy-start | bytes 98308
  3.2 0.8 %copy-start.2 = (f32[8,8,128]{2,1,0:T(8,128)S(1)}, f32[8,8,128]{2,1,0:T(8,128)}, u32[]{:S(2)}) copy-start(f32[8,8,128]{2,1,0:T(8,128)} %recharge_in.1) | copy-start | bytes 98308
  4.0 0.8 %copy-start.3 = (s32[8,8,128]{2,1,0:T(8,128)S(1)}, s32[8,8,128]{2,1,0:T(8,128)}, u32[]{:S(2)}) copy-start(s32[8,8,128]{2,1,0:T(8,128)} %soil_zone_in.1) | copy-start | bytes 98308
  4.8 0.8 %copy-start.4 = (s32[8,8,128]{2,1,0:T(8,128)S(1)}, s32[8,8,128]{2,1,0:T(8,128)}, u32[]{:S(2)}) copy-start(s32[8,8,128]{2,1,0:T(8,128)} %mineral_zone_in.1) | copy-start | bytes 98308

commit v3 on v2

--- a/solution.py
+++ b/solution.py
@@ -182,7 +182,7 @@
     species = len(moved)
     rates = [table_lookup(labels, [rate_table[z, m] for z in range(zones)]) for m in range(minerals)]
     base = [
-        weighted([stoich[c, m] for c in range(species)], moved) - log_equil[m]
+        weighted([stoich[m, c] for c in range(species)], moved) - log_equil[m]
         for m in range(minerals)
     ]
     extent = None
@@ -202,7 +202,7 @@
         step = [newton_damping * (start[m] - correction[m]) for m in range(minerals)]
         extent = [-step[m] if extent is None else extent[m] - step[m] for m in range(minerals)]
     return [
-        moved[c] + weighted([stoich[c, m] for m in range(minerals)], extent)
+        moved[c] + weighted([stoich[m, c] for m in range(minerals)], extent)
         for c in range(species)
     ]
 
@@ -214,15 +214,20 @@
     previous_head_in,
     recharge_in,
     soil_zone_in,
+    soil_cond_in,
+    soil_store_in,
+    species_in,
+    mineral_zone_in,
+    rate_table_in,
+    stoich_in,
+    log_equil_in,
+    head_out,
+    species_out,
     soil_cond,
     soil_store,
-    species_in,
-    mineral_zone_in,
     rate_table,
     stoich,
     log_equil,
-    head_out,
-    species_out,
     previous_head,
     recharge,
     soil_zone,
@@ -296,6 +301,11 @@
                 (species_in, species),
                 (species_in.at[:, :, :, columns_of(s)], conc.at[pl.ds(group * s, group)]),
                 (mineral_zone_in, mineral_zone),
+                (soil_store_in, soil_store),
+                (soil_cond_in, soil_cond),
+                (rate_table_in, rate_table),
+                (stoich_in, stoich),
+                (log_equil_in, log_equil),
             )
         )
     ]
@@ -310,7 +320,7 @@
     for peer in peers:
         pl.semaphore_signal(barrier, inc=1, device_id=peer, device_id_type=MESH)
 
-    for copy in loads[:3]:
+    for copy in loads[:3] + loads[6:7]:
         copy.wait()
     zone = soil_zone[...]
     field[0] = table_lookup(zone, soil_store) * previous_head[...] + recharge[...]
@@ -370,6 +380,8 @@
                 beside(rows, k),
             )
 
+    for copy in loads[7:]:
+        copy.wait()
     for copy in halo:
         copy.wait_recv()
 
@@ -428,11 +440,11 @@
         totals = jnp.broadcast_to(jnp.sum(partial, axis=1, keepdims=True), (lines, 256))
         return [totals[k : k + 1] for k in range(len(pairs))]
 
-    species_count, mineral_count = stoich.shape
+    mineral_count, species_count = stoich.shape
 
     def fill_gram():
         columns = [
-            [stoich[c, m] for c in range(species_count)] for m in range(mineral_count)
+            [stoich[m, c] for c in range(species_count)] for m in range(mineral_count)
         ]
         for i in range(mineral_count):
             for j in range(i + 1):
@@ -567,8 +579,9 @@
     group, layers, _, width = species.shape
     total = group * sp_count
     minerals = arrays[8].shape[1]
+    arrays = arrays[:8] + (arrays[8].T,) + arrays[9:]
+    tables = arrays[3:5] + arrays[7:]
     vmem = pl.BlockSpec(memory_space=pltpu.VMEM)
-    smem = pl.BlockSpec(memory_space=pltpu.SMEM)
     hbm = pl.BlockSpec(memory_space=pltpu.HBM)
     cells = (layers, 8, 128)
 
@@ -582,9 +595,10 @@
                 jax.ShapeDtypeStruct(cells, jnp.float32),
                 jax.ShapeDtypeStruct(species.shape, jnp.float32),
             ),
-            in_specs=[hbm, hbm, hbm, smem, smem, hbm, hbm, smem, smem, smem],
+            in_specs=[hbm] * 10,
             out_specs=(vmem, hbm),
             scratch_shapes=[
+                *[pltpu.SMEM(table.shape, jnp.float32) for table in tables],
                 floats(*cells),
                 floats(*cells),
                 pltpu.VMEM(cells, jnp.int32),
@@ -608,7 +622,7 @@
                 floats(total, *cells),
                 floats(total, *cells),
                 pltpu.SMEM((minerals, minerals), jnp.float32),
-                pltpu.SemaphoreType.DMA((6,)),
+                pltpu.SemaphoreType.DMA((11,)),
                 pltpu.SemaphoreType.DMA((8,)),
                 pltpu.SemaphoreType.DMA((8,)),
                 pltpu.SemaphoreType.DMA((4,)),
@@ -618,7 +632,7 @@
                 pltpu.SemaphoreType.DMA((3,)),
             ],
             compiler_params=pltpu.CompilerParams(
-                collective_id=0, has_side_effects=True, vmem_limit_bytes=48 * 1024 * 1024
+                collective_id=0, has_side_effects=True, vmem_limit_bytes=60 * 1024 * 1024
             ),
         )(*arrays)
     )

time: 47.4 us -> 43.8 us (0.924)
  local copies, waits for them, and re-layouts: 6.19 us -> 3.14 us
    unnamed x21 -> x2, local copies, waits for them, and re-layouts: 6.19 us -> 3.14 us
where the time goes in v3:
time: 43.8 us; the launch traced here: 43.6 us
  Pallas kernels  39.8 us (91%)
  local copies, waits for them, and re-layouts  3.14 us (7%)
  between operations  0.64 us (1%)
    pallas_call x1, Pallas kernels, per_device(): pl.pallas_call(functools.partial(step_kernel, gx_count, sp_count, inner),...  39.8 us
    unnamed x2, local copies, waits for them, and re-layouts  3.14 us

profile of v3, /device:TPU:1, one launch (start us, length us, event | category | flops | bytes accessed | tf_op | source)
XLA Modules:
  0.0 43.6 jit_solution(15130394592198573452)
XLA Ops:
  0.6 39.8 %shard_map.113 = (f32[8,8,128]{2,1,0:T(8,128)}, f32[3,8,8,512]{3,2,1,0:T(8,128)}) custom-call(f32[8,8,128]{2,1,0:T(8,128)} %previous_head_in.1, f32[8,8,128]{2,1,0:T(8,128)} %recharge_in.1, s32[8,8,128]{2,1,0:T(8,128)} %soil_zone_in.1, f32[8]{0:T(128)} %soil_cond_in.1, f32[8]{0:T(128)} %soil_store_in.1, f32[3,8,8,512]{3,2,1,0:T(8,128)} %species_in.1, ...), custom_call_target="tpu_custom_call" | custom-call | tf_op jit(solution)/shard_map/pallas_call | solution.py:592
  40.4 1.4 %copy.14 = f32[8,8,128]{2,1,0:T(8,128)} copy(f32[8,8,128]{2,1,0:T(8,128)} %get-tuple-element.4) | data formatting | bytes 65536
  41.8 1.8 %copy.15 = f32[3,8,8,512]{3,2,1,0:T(8,128)} copy(f32[3,8,8,512]{3,2,1,0:T(8,128)} %get-tuple-element.5) | data formatting | bytes 786432

commit v4 on v3

--- a/solution.py
+++ b/solution.py
@@ -237,10 +237,8 @@
     rows_in,
     edge_out,
     edge_in,
-    near_0,
-    far_0,
-    near_1,
-    far_1,
+    gathered_0,
+    gathered_1,
     conc,
     ends_out,
     ends_in,
@@ -262,14 +260,29 @@
 ):
     g = lax.axis_index("gx")
     s = lax.axis_index("sp")
-    outer = gx_count // inner
-    low, high = g % inner, g // inner
-    plane = high * sp_count + s
-    near_peers = [(high * inner + (low + k) % inner, s) for k in range(1, inner)]
-    far_peers = [
-        (((high + k // sp_count) % outer) * inner + low, (s + k % sp_count) % sp_count)
-        for k in range(1, outer * sp_count)
+    cores, across = 2, inner // 2
+    down = gx_count // inner
+    core, x, y = lax.rem(g, cores), lax.rem(lax.div(g, cores), across), lax.div(g, inner)
+    at_core = [lax.rem(core + k, cores) for k in range(cores)]
+    at_x = [lax.rem(x + k, across) * cores for k in range(across)]
+    at_y = [lax.rem(y + k, down) * inner for k in range(down)]
+    at_z = [lax.rem(s + k, sp_count) for k in range(sp_count)]
+    at_gx = [[[a + b + c for c in at_core] for b in at_x] for a in at_y]
+
+    def hops(k, count):
+        return min(k, count - k)
+
+    steps = [
+        (hops(i, down) + hops(j, across) + hops(m, sp_count), k, i, j, m)
+        for i in range(down)
+        for j in range(across)
+        for k in range(cores)
+        for m in range(sp_count)
+    ][1:]
+    everyone = [
+        (at_gx[i][j][k], at_z[m]) for _, k, i, j, m in sorted(steps, reverse=True)
     ]
+    slot = g * sp_count + s
     group = species_in.shape[0]
     layers = species_in.shape[1]
 
@@ -313,11 +326,8 @@
         copy.start()
 
     offsets = [(rows, columns) for rows in (-1, 0, 1) for columns in (-1, 0, 1) if (rows, columns) != (0, 0)]
-    others = [k for k in range(2, sp_count - 1)]
     barrier = pltpu.get_barrier_semaphore()
-    peers = [beside(*offset) for offset in offsets] + near_peers + far_peers
-    peers += [beside(rows, k) for rows in (-1, 1) for k in others]
-    for peer in peers:
+    for peer in everyone:
         pl.semaphore_signal(barrier, inc=1, device_id=peer, device_id_type=MESH)
 
     for copy in loads[:3] + loads[6:7]:
@@ -330,7 +340,7 @@
     pick = (lane == jnp.where(line < 8, line, line + 112)).astype(jnp.float32)
     edge_out[...] = column_edges(pick, field[...].reshape(128, 128))
 
-    pl.semaphore_wait(barrier, len(peers))
+    pl.semaphore_wait(barrier, len(everyone))
     halo = []
     for number, (rows, columns) in enumerate(offsets):
         if columns == 0:
@@ -416,29 +426,27 @@
 
     sends = []
 
-    def exchange(buffer, slot, value, to_peers, number, meanwhile):
-        buffer[slot] = value
-        for peer in to_peers:
-            remote(buffer.at[slot], buffer.at[slot], sum_send.at[number], sum_recv.at[number], peer)
-        if meanwhile is not None:
-            meanwhile()
-        all_others = buffer.at[pl.ds(0, len(to_peers))]
-        pltpu.make_async_copy(all_others, all_others, sum_recv.at[number]).wait()
-        sends.append(pltpu.make_async_copy(all_others, all_others, sum_send.at[number]))
-        return jnp.sum(buffer[...], axis=0)
-
-    def global_sums(pairs, near, far, number, first_work, second_work):
-        lines = near.shape[1]
-        index = lax.broadcasted_iota(jnp.int32, (lines, 128), 0)
+    def global_sums(pairs, gathered, number, meanwhile):
+        lines = -(-len(pairs) // 8) * 8
+        row = lax.broadcasted_iota(jnp.int32, (lines, 128), 0)
+        lane = lax.broadcasted_iota(jnp.int32, (lines, 128), 1)
         partial = jnp.zeros((lines, 128), jnp.float32)
         for position, (left, right) in enumerate(pairs):
             product = left[:, 8:16, :128] * right[:, 8:16, :128]
             total = jnp.sum(jnp.sum(product, axis=0), axis=0, keepdims=True)
-            partial = jnp.where(index == position, total, partial)
-        partial = exchange(near, low, partial, near_peers, number, first_work)
-        partial = exchange(far, plane, partial, far_peers, number + 1, second_work)
-        totals = jnp.broadcast_to(jnp.sum(partial, axis=1, keepdims=True), (lines, 256))
-        return [totals[k : k + 1] for k in range(len(pairs))]
+            partial = jnp.where(row == position, total, partial)
+        totals = jnp.sum(partial, axis=1, keepdims=True)
+        gathered[slot] = jnp.sum(jnp.where(row == lane, totals, 0.0), axis=0, keepdims=True)
+        for peer in everyone:
+            remote(
+                gathered.at[slot], gathered.at[slot], sum_send.at[number], sum_recv.at[number], peer
+            )
+        meanwhile()
+        all_others = gathered.at[pl.ds(0, len(everyone))]
+        pltpu.make_async_copy(all_others, all_others, sum_recv.at[number]).wait()
+        sends.append(pltpu.make_async_copy(all_others, all_others, sum_send.at[number]))
+        total = jnp.sum(gathered[...], axis=0)
+        return [jnp.broadcast_to(total[:, k : k + 1], (1, 256)) for k in range(len(pairs))]
 
     mineral_count, species_count = stoich.shape
 
@@ -483,7 +491,7 @@
     for k in range(BLOCK):
         powers.append(apply_flow(powers[-1], storage, faces))
     pairs = [(powers[k // 2], powers[(k + 1) // 2]) for k in range(2 * BLOCK + 1)]
-    moments = global_sums(pairs, near_0, far_0, 0, fill_gram, None)
+    moments = global_sums(pairs, gathered_0, 0, fill_gram)
     change, residual, direction = cg_block(moments, moments, moments, least, most, True)
     head = combine(change, [powers])
     residual = combine(residual, [powers])
@@ -498,7 +506,7 @@
     pairs = [(r_powers[k // 2], r_powers[(k + 1) // 2]) for k in range(4)]
     pairs += [(p_powers[(k + 1) // 2], r_powers[k // 2]) for k in range(5)]
     pairs += [(p_powers[k // 2], p_powers[(k + 1) // 2]) for k in range(6)]
-    moments = global_sums(pairs, near_1, far_1, 2, place_species, None)
+    moments = global_sums(pairs, gathered_1, 1, place_species)
     change, _, _ = cg_block(moments[:4], moments[4:9], moments[9:], least, most, False)
     head = head + combine(change, [p_powers, r_powers])
 
@@ -574,7 +582,6 @@
 def per_device(mesh, *arrays):
     gx_count, sp_count = mesh.shape["gx"], mesh.shape["sp"]
     inner = min(8, gx_count // 2)
-    far_count = gx_count // inner * sp_count
     species = arrays[5]
     group, layers, _, width = species.shape
     total = group * sp_count
@@ -608,10 +615,8 @@
                 floats(2, 2, *cells),
                 floats(16, 128),
                 floats(3, 16, 128),
-                floats(inner, 8, 128),
-                floats(far_count, 8, 128),
-                floats(inner, 16, 128),
-                floats(far_count, 16, 128),
+                floats(gx_count * sp_count, 1, 128),
+                floats(gx_count * sp_count, 1, 128),
                 floats(total, *cells),
                 floats(2, group, layers, width),
                 floats(2, total, layers, 128),
@@ -625,8 +630,8 @@
                 pltpu.SemaphoreType.DMA((11,)),
                 pltpu.SemaphoreType.DMA((8,)),
                 pltpu.SemaphoreType.DMA((8,)),
-                pltpu.SemaphoreType.DMA((4,)),
-                pltpu.SemaphoreType.DMA((4,)),
+                pltpu.SemaphoreType.DMA((2,)),
+                pltpu.SemaphoreType.DMA((2,)),
                 pltpu.SemaphoreType.DMA((3,)),
                 pltpu.SemaphoreType.DMA((3,)),
                 pltpu.SemaphoreType.DMA((3,)),

time: 43.8 us -> 40.9 us (0.934)
  Pallas kernels: 39.8 us -> 36.8 us
    pallas_call x1, Pallas kernels: 39.8 us -> 36.8 us  [per_device(): pl.pallas_call(functools.partial(step_kernel, gx_count, sp_count, inner),...]
where the time goes in v4:
time: 40.9 us; the launch traced here: 40.6 us
  Pallas kernels  36.8 us (90%)
  local copies, waits for them, and re-layouts  3.14 us (8%)
  between operations  0.64 us (2%)
    pallas_call x1, Pallas kernels, per_device(): pl.pallas_call(functools.partial(step_kernel, gx_count, sp_count, inner),...  36.8 us
    unnamed x2, local copies, waits for them, and re-layouts  3.14 us

profile of v4, /device:TPU:1, one launch (start us, length us, event | category | flops | bytes accessed | tf_op | source)
XLA Modules:
  0.0 40.6 jit_solution(8883129249063236897)
XLA Ops:
  0.6 36.8 %shard_map.113 = (f32[8,8,128]{2,1,0:T(8,128)}, f32[3,8,8,512]{3,2,1,0:T(8,128)}) custom-call(f32[8,8,128]{2,1,0:T(8,128)} %previous_head_in.1, f32[8,8,128]{2,1,0:T(8,128)} %recharge_in.1, s32[8,8,128]{2,1,0:T(8,128)} %soil_zone_in.1, f32[8]{0:T(128)} %soil_cond_in.1, f32[8]{0:T(128)} %soil_store_in.1, f32[3,8,8,512]{3,2,1,0:T(8,128)} %species_in.1, ...), custom_call_target="tpu_custom_call" | custom-call | tf_op jit(solution)/shard_map/pallas_call | solution.py:599
  37.4 1.4 %copy.14 = f32[8,8,128]{2,1,0:T(8,128)} copy(f32[8,8,128]{2,1,0:T(8,128)} %get-tuple-element.4) | data formatting | bytes 65536
  38.8 1.8 %copy.15 = f32[3,8,8,512]{3,2,1,0:T(8,128)} copy(f32[3,8,8,512]{3,2,1,0:T(8,128)} %get-tuple-element.5) | data formatting | bytes 786432

commit v5 on v4

--- a/solution.py
+++ b/solution.py
@@ -445,7 +445,11 @@
         all_others = gathered.at[pl.ds(0, len(everyone))]
         pltpu.make_async_copy(all_others, all_others, sum_recv.at[number]).wait()
         sends.append(pltpu.make_async_copy(all_others, all_others, sum_send.at[number]))
-        total = jnp.sum(gathered[...], axis=0)
+        total = gathered[...]
+        while total.shape[0] > 1:
+            half = total.shape[0] // 2
+            total = total[:half] + total[half:]
+        total = total[0]
         return [jnp.broadcast_to(total[:, k : k + 1], (1, 256)) for k in range(len(pairs))]
 
     mineral_count, species_count = stoich.shape
@@ -579,6 +583,23 @@
     pltpu.make_async_copy(once, once, result_sem.at[2]).wait()
 
 
+def hand_over(head, species, head_out, species_out, head_held, species_held, load_sem, store_sem):
+    parts = [(head, head_held, head_out)]
+    for k in range(species.shape[0]):
+        parts.append((species.at[k], species_held.at[k], species_out.at[k]))
+    loads, stores = [], []
+    for number, (source, held, target) in enumerate(parts):
+        loads.append(pltpu.make_async_copy(source, held, load_sem.at[number]))
+        stores.append(pltpu.make_async_copy(held, target, store_sem.at[number]))
+    for copy in loads:
+        copy.start()
+    for load, store in zip(loads, stores):
+        load.wait()
+        store.start()
+    for copy in stores:
+        copy.wait()
+
+
 def per_device(mesh, *arrays):
     gx_count, sp_count = mesh.shape["gx"], mesh.shape["sp"]
     inner = min(8, gx_count // 2)
@@ -595,7 +616,7 @@
     def floats(*shape):
         return pltpu.VMEM(shape, jnp.float32)
 
-    return tuple(
+    results = (
         pl.pallas_call(
             functools.partial(step_kernel, gx_count, sp_count, inner),
             out_shape=(
@@ -642,6 +663,21 @@
         )(*arrays)
     )
 
+    return tuple(
+        pl.pallas_call(
+            hand_over,
+            out_shape=tuple(jax.ShapeDtypeStruct(r.shape, r.dtype) for r in results),
+            in_specs=[hbm, hbm],
+            out_specs=(hbm, hbm),
+            scratch_shapes=[
+                *[floats(*r.shape) for r in results],
+                pltpu.SemaphoreType.DMA((1 + group,)),
+                pltpu.SemaphoreType.DMA((1 + group,)),
+            ],
+            compiler_params=pltpu.CompilerParams(vmem_limit_bytes=60 * 1024 * 1024),
+        )(*results)
+    )
+
 
 def solution(mesh):
     cells = P(None, "gx", "sp")

time: 40.9 us -> 39.2 us (0.958)
  local copies, waits for them, and re-layouts: 3.14 us -> 0 us
  Pallas kernels: 36.8 us -> 38.4 us
    unnamed x2 -> x0, local copies, waits for them, and re-layouts: 3.14 us -> none
    pallas_call x0 -> x1, Pallas kernels: none -> 1.77 us  [per_device(): pl.pallas_call(hand_over, out_shape=tuple((jax.ShapeDtypeStruct(r.shape,...]
where the time goes in v5:
time: 39.2 us; the launch traced here: 39 us
  Pallas kernels  38.4 us (98%)
  between operations  0.64 us (2%)
    pallas_call x1, Pallas kernels, per_device(): pl.pallas_call(functools.partial(step_kernel, gx_count, sp_count, inner),...  36.6 us
    pallas_call x1, Pallas kernels, per_device(): pl.pallas_call(hand_over, out_shape=tuple((jax.ShapeDtypeStruct(r.shape,...  1.77 us

profile of v5, /device:TPU:1, one launch (start us, length us, event | category | flops | bytes accessed | tf_op | source)
XLA Modules:
  0.0 39.0 jit_solution(9410204835018240567)
XLA Ops:
  0.6 36.6 %shard_map.113 = (f32[8,8,128]{2,1,0:T(8,128)}, f32[3,8,8,512]{3,2,1,0:T(8,128)}) custom-call(f32[8,8,128]{2,1,0:T(8,128)} %previous_head_in.1, f32[8,8,128]{2,1,0:T(8,128)} %recharge_in.1, s32[8,8,128]{2,1,0:T(8,128)} %soil_zone_in.1, f32[8]{0:T(128)} %soil_cond_in.1, f32[8]{0:T(128)} %soil_store_in.1, f32[3,8,8,512]{3,2,1,0:T(8,128)} %species_in.1, ...), custom_call_target="tpu_custom_call" | custom-call | tf_op jit(solution)/shard_map/pallas_call | solution.py:620
  37.2 1.8 %shard_map.114 = (f32[8,8,128]{2,1,0:T(8,128)}, f32[3,8,8,512]{3,2,1,0:T(8,128)}) custom-call(f32[8,8,128]{2,1,0:T(8,128)} %get-tuple-element.4.head, f32[3,8,8,512]{3,2,1,0:T(8,128)} %get-tuple-element.5.species), custom_call_target="tpu_custom_call" | custom-call | tf_op jit(solution)/shard_map/pallas_call | solution.py:667

commit v6 on v5

--- a/solution.py
+++ b/solution.py
@@ -8,7 +8,9 @@
 from jax.sharding import PartitionSpec as P
 
 NEWTON = 2
-BLOCK = 3
+SHIFTS = (0.5, 0.125, 1.0, 0.25, 1.0, 0.0625)
+CHUNK = 2
+PIECE = 2
 
 time_step = 0.05
 dispersion = 0.5
@@ -77,54 +79,113 @@
     return result
 
 
-def add_scaled(left, scale, right):
-    total = dict(left)
-    for key, value in right.items():
-        term = scale * value
-        total[key] = total[key] + term if key in total else term
-    return total
-
-
-def cg_block(rr, pr, pp, least, most, same):
-    one = jnp.ones_like(least)
-    direction = {(0, 0): one}
-    residual = {(0 if same else 1, 0): one}
-    change = {}
-    live = None
-    for step in range(BLOCK):
-        alpha = (pr if step == 0 else rr)[0] / jnp.maximum(pp[1], 1e-30)
-        alpha = jnp.clip(alpha, least, most)
-        if live is not None:
-            alpha = jnp.where(live, alpha, 0.0)
-        change = add_scaled(change, alpha, direction)
-        image = {(part, power + 1): value for (part, power), value in direction.items()}
-        residual = add_scaled(residual, -alpha, image)
-        if len(pp) < 3 or len(pr) < 2:
-            break
-        square = alpha * alpha
-        count = min(len(rr), len(pr) - 1, len(pp) - 2)
-        next_rr = [rr[k] - 2.0 * alpha * pr[k + 1] + square * pp[k + 2] for k in range(count)]
-        count = min(len(pr), len(pp) - 1)
-        next_pr = [pr[k] - alpha * pp[k + 1] for k in range(count)]
-        above = next_rr[0] > 1e-6 * (rr[0] + square * pp[2])
-        live = above if live is None else live & above
-        beta = jnp.where(live, next_rr[0] / jnp.maximum(rr[0], 1e-37), 0.0)
-        direction = add_scaled(residual, beta, direction)
-        count = min(len(next_rr), len(next_pr))
-        next_pp = [
-            next_rr[k] + 2.0 * beta * next_pr[k] + beta * beta * pp[k] for k in range(count)
-        ]
-        pr = [next_rr[k] + beta * next_pr[k] for k in range(count)]
-        rr, pp = next_rr, next_pp
-    return change, residual, direction
-
-
-def combine(polynomial, parts):
-    total = None
-    for (part, power), value in sorted(polynomial.items()):
-        term = value[None] * parts[part][power]
-        total = term if total is None else total + term
-    return total
+def exact_sum(left, right):
+    total = left + right
+    part = total - left
+    return total, (left - (total - part)) + (right - part)
+
+
+def split(value):
+    wide = 4097.0 * value
+    high = wide - (wide - value)
+    return high, value - high
+
+
+def paired(high, low):
+    total = high + low
+    return total, low - (total - high)
+
+
+def pair_add(left, right):
+    total, error = exact_sum(left[0], right[0])
+    return paired(total, error + (left[1] + right[1]))
+
+
+def pair_minus(left, right):
+    return pair_add(left, (-right[0], -right[1]))
+
+
+def pair_times(left, right):
+    left_high, left_low = split(left[0])
+    right_high, right_low = split(right[0])
+    product = left[0] * right[0]
+    error = left_high * right_high - product
+    error = error + left_high * right_low + left_low * right_high + left_low * right_low
+    return paired(product, error + (left[0] * right[1] + left[1] * right[0]))
+
+
+def pair_inverse(value):
+    guess = 1.0 / value[0]
+    none = jnp.zeros_like(guess)
+    rest = pair_minus((none + 1.0, none), pair_times(value, (guess, none)))
+    return paired(guess, guess * (rest[0] + rest[1]))
+
+
+def halved(total, error):
+    half = total.shape[0] // 2
+    total, more = exact_sum(total[:half], total[half:])
+    return total, error[:half] + error[half:] + more
+
+
+def inner_product(left, right):
+    total = left[0] * right[0]
+    error = left[0] * right[1] + left[1] * right[0] + left[1] * right[1]
+    while total.shape[0] > 1:
+        total, error = halved(total, error)
+    return total[0], error[0]
+
+
+def merge_rows(pairs):
+    row = lax.broadcasted_iota(jnp.int32, (8, 128), 0)
+    for shift in (4, 2, 1):
+        keep = (row % (2 * shift)) < shift
+        merged = []
+        for left, right in zip(pairs[:shift], pairs[shift:]):
+            ends = []
+            for part in range(2):
+                ends.append(
+                    (
+                        jnp.where(keep, left[part], pltpu.roll(right[part], shift, 0)),
+                        jnp.where(keep, pltpu.roll(left[part], 8 - shift, 0), right[part]),
+                    )
+                )
+            total, error = exact_sum(*ends[0])
+            merged.append((total, error + (ends[1][0] + ends[1][1])))
+        pairs = merged
+    return pairs[0]
+
+
+def solve_krylov(gram):
+    size = len(SHIFTS)
+    matrix = {}
+    for i in range(size):
+        for j in range(i, size):
+            after = pair_add(gram[i, j + 1], gram[min(i + 1, j), max(i + 1, j)])
+            for shift in (SHIFTS[i], SHIFTS[j]):
+                after = pair_add(after, (shift * gram[i, j][0], shift * gram[i, j][1]))
+            matrix[j, i] = after
+    right = [gram[0, i] for i in range(size)]
+    first = [gram[k, k][0] for k in range(size)]
+    inverse, lower = [None] * size, {}
+    for k in range(size):
+        pivot = matrix[k, k]
+        usable = pivot[0] > 8e-12 * first[k]
+        inverse[k] = tuple(jnp.where(usable, part, 0.0) for part in pair_inverse(pivot))
+        for i in range(k + 1, size):
+            lower[i, k] = pair_times(matrix[i, k], inverse[k])
+        for i in range(k + 1, size):
+            right[i] = pair_minus(right[i], pair_times(lower[i, k], right[k]))
+            for j in range(k + 1, i + 1):
+                matrix[i, j] = pair_minus(
+                    matrix[i, j], pair_times(lower[i, k], matrix[j, k])
+                )
+    answer = [None] * size
+    for k in reversed(range(size)):
+        value = pair_times(right[k], inverse[k])[0]
+        for i in range(k + 1, size):
+            value = value - lower[i, k][0] * answer[i]
+        answer[k] = value
+    return [2.0 * value for value in answer]
 
 
 def column_edges(pick, block):
@@ -237,8 +298,7 @@
     rows_in,
     edge_out,
     edge_in,
-    gathered_0,
-    gathered_1,
+    gathered,
     conc,
     ends_out,
     ends_in,
@@ -246,7 +306,6 @@
     sides_in,
     beside_conc,
     weights,
-    moved,
     reacted,
     gram_table,
     load_sem,
@@ -304,6 +363,7 @@
         copy.start()
         return copy
 
+    middle = pl.ds(1, layers)
     loads = [
         pltpu.make_async_copy(source, target, load_sem.at[number])
         for number, (source, target) in enumerate(
@@ -312,7 +372,7 @@
                 (previous_head_in, previous_head),
                 (recharge_in, recharge),
                 (species_in, species),
-                (species_in.at[:, :, :, columns_of(s)], conc.at[pl.ds(group * s, group)]),
+                (species_in.at[:, :, :, columns_of(s)], conc.at[pl.ds(group * s, group), middle]),
                 (mineral_zone_in, mineral_zone),
                 (soil_store_in, soil_store),
                 (soil_cond_in, soil_cond),
@@ -332,6 +392,9 @@
 
     for copy in loads[:3] + loads[6:7]:
         copy.wait()
+    for number in range(group * sp_count):
+        conc[number, 0] = jnp.zeros((8, 128), jnp.float32)
+        conc[number, layers + 1] = jnp.zeros((8, 128), jnp.float32)
     zone = soil_zone[...]
     field[0] = table_lookup(zone, soil_store) * previous_head[...] + recharge[...]
     field[1] = zone.astype(jnp.float32)
@@ -359,7 +422,7 @@
         to = (s + k) % sp_count
         remote(
             species.at[:, :, :, columns_of(to)],
-            conc.at[mine],
+            conc.at[mine, middle],
             spread_send.at[0],
             spread_recv.at[0],
             (g, to),
@@ -416,41 +479,11 @@
     storage = jnp.where(inside, table_lookup(wide[1], soil_store), 0.0)
     faces = six_faces(conduct)
 
-    store_least, store_most, cond_most = soil_store[0], soil_store[0], soil_cond[0]
+    store_most, cond_most = soil_store[0], soil_cond[0]
     for level in range(1, soil_store.shape[0]):
-        store_least = jnp.minimum(store_least, soil_store[level])
         store_most = jnp.maximum(store_most, soil_store[level])
         cond_most = jnp.maximum(cond_most, soil_cond[level])
-    most = 1.0 / jnp.full((1, 256), store_least, jnp.float32)
-    least = 1.0 / jnp.full((1, 256), store_most + 12.0 * cond_most, jnp.float32)
-
-    sends = []
-
-    def global_sums(pairs, gathered, number, meanwhile):
-        lines = -(-len(pairs) // 8) * 8
-        row = lax.broadcasted_iota(jnp.int32, (lines, 128), 0)
-        lane = lax.broadcasted_iota(jnp.int32, (lines, 128), 1)
-        partial = jnp.zeros((lines, 128), jnp.float32)
-        for position, (left, right) in enumerate(pairs):
-            product = left[:, 8:16, :128] * right[:, 8:16, :128]
-            total = jnp.sum(jnp.sum(product, axis=0), axis=0, keepdims=True)
-            partial = jnp.where(row == position, total, partial)
-        totals = jnp.sum(partial, axis=1, keepdims=True)
-        gathered[slot] = jnp.sum(jnp.where(row == lane, totals, 0.0), axis=0, keepdims=True)
-        for peer in everyone:
-            remote(
-                gathered.at[slot], gathered.at[slot], sum_send.at[number], sum_recv.at[number], peer
-            )
-        meanwhile()
-        all_others = gathered.at[pl.ds(0, len(everyone))]
-        pltpu.make_async_copy(all_others, all_others, sum_recv.at[number]).wait()
-        sends.append(pltpu.make_async_copy(all_others, all_others, sum_send.at[number]))
-        total = gathered[...]
-        while total.shape[0] > 1:
-            half = total.shape[0] // 2
-            total = total[:half] + total[half:]
-        total = total[0]
-        return [jnp.broadcast_to(total[:, k : k + 1], (1, 256)) for k in range(len(pairs))]
+    scale = 2.0 / jnp.full((1, 256), store_most + 12.0 * cond_most, jnp.float32)
 
     mineral_count, species_count = stoich.shape
 
@@ -466,7 +499,7 @@
                 gram_table[i, j] = terms[0]
 
     def place_species():
-        whole = conc.at[pl.ds(0, group * (sp_count - 1))]
+        whole = conc.at[pl.ds(0, group * (sp_count - 1)), middle]
         pltpu.make_async_copy(whole, whole, spread_recv.at[0]).wait()
         part = sides_in.at[pl.ds(0, sp_count - 1)]
         pltpu.make_async_copy(part, part, spread_recv.at[1]).wait()
@@ -482,7 +515,7 @@
         shape = (group, layers, 8, 128)
         for block in range(sp_count):
             part = pl.ds(group * block, group)
-            center = conc[part]
+            center = conc[part, middle]
             edges = spread_edges(sides_in[block][:, :tiles], place).reshape(shape)
             upper = jnp.broadcast_to(ends_in[0, part][:, :, None, :], shape)
             under = jnp.broadcast_to(ends_in[1, part][:, :, None, :], shape)
@@ -491,31 +524,57 @@
             beside_conc[2, part] = jnp.where(lane == 127, edges, shifted(center, 1, 3))
             beside_conc[3, part] = jnp.where(lane == 0, edges, shifted(center, -1, 3))
 
-    powers = [source]
-    for k in range(BLOCK):
-        powers.append(apply_flow(powers[-1], storage, faces))
-    pairs = [(powers[k // 2], powers[(k + 1) // 2]) for k in range(2 * BLOCK + 1)]
-    moments = global_sums(pairs, gathered_0, 0, fill_gram)
-    change, residual, direction = cg_block(moments, moments, moments, least, most, True)
-    head = combine(change, [powers])
-    residual = combine(residual, [powers])
-    direction = combine(direction, [powers])
-
-    p_powers = [direction]
-    for k in range(BLOCK):
-        p_powers.append(apply_flow(p_powers[-1], storage, faces))
-    r_powers = [residual]
-    for k in range(BLOCK - 1):
-        r_powers.append(apply_flow(r_powers[-1], storage, faces))
-    pairs = [(r_powers[k // 2], r_powers[(k + 1) // 2]) for k in range(4)]
-    pairs += [(p_powers[(k + 1) // 2], r_powers[k // 2]) for k in range(5)]
-    pairs += [(p_powers[k // 2], p_powers[(k + 1) // 2]) for k in range(6)]
-    moments = global_sums(pairs, gathered_1, 1, place_species)
-    change, _, _ = cg_block(moments[:4], moments[4:9], moments[9:], least, most, False)
-    head = head + combine(change, [p_powers, r_powers])
-
     def own(values):
         return values[:, 8:16, :128]
+
+    basis = [source]
+    for shift in SHIFTS:
+        image = scale[None] * apply_flow(basis[-1], storage, faces)
+        basis.append(image - shift * basis[-1])
+    parts = [split(own(vector)) for vector in basis]
+    size = len(SHIFTS)
+    places = [(i, j) for i in range(size) for j in range(i, size + 1)]
+    products = [inner_product(parts[i], parts[j]) for i, j in places]
+    lines = 32
+    blank = jnp.zeros((8, 128), jnp.float32)
+    products += [(blank, blank)] * (lines - len(products))
+    rows = [merge_rows(products[first : first + 8]) for first in range(0, lines, 8)]
+    rows = [row[0] for row in rows] + [row[1] for row in rows]
+    table = jnp.concatenate(rows + [blank] * (16 - len(rows)), axis=0).T
+    error = jnp.zeros_like(table)
+    while table.shape[0] > 8:
+        table, error = halved(table, error)
+    for shift in (4, 2, 1):
+        table, more = exact_sum(table, pltpu.roll(table, shift, 0))
+        error = error + pltpu.roll(error, shift, 0) + more
+    lane = lax.broadcasted_iota(jnp.int32, (8, 128), 1)
+    table = jnp.where(lane < 2 * lines, table, pltpu.roll(error, 2 * lines, 1))
+    gathered[slot] = table[:1]
+    for peer in everyone:
+        remote(gathered.at[slot], gathered.at[slot], sum_send.at[0], sum_recv.at[0], peer)
+    fill_gram()
+    place_species()
+    all_others = gathered.at[pl.ds(0, len(everyone))]
+    pltpu.make_async_copy(all_others, all_others, sum_recv.at[0]).wait()
+    table = gathered[...]
+    error = jnp.zeros_like(table)
+    while table.shape[0] > 1:
+        table, error = halved(table, error)
+    table = jnp.broadcast_to(table[0], (8, 128))
+    error = jnp.broadcast_to(error[0], (8, 128))
+    error = error + pltpu.roll(table, 128 - 2 * lines, 1) + pltpu.roll(table, 128 - lines, 1)
+    high, low = paired(table, error)
+    entries = {
+        place: tuple(
+            jnp.broadcast_to(part[:1, k : k + 1], (1, 128)) for part in (high, low)
+        )
+        for k, place in enumerate(places)
+    }
+    answer = solve_krylov(entries)
+    head = None
+    for value, vector in zip(answer, basis):
+        term = (scale * jnp.concatenate([value, value], axis=1))[None] * vector
+        head = term if head is None else head + term
 
     head_out[...] = own(head)
     kept = jnp.ones_like(own(head))
@@ -524,17 +583,10 @@
         velocity = face * (own(head) - own(head_beside))
         kept = kept - time_step * (jnp.maximum(velocity, 0.0) + dispersion * face)
         weights[number] = time_step * (dispersion * face - jnp.minimum(velocity, 0.0))
-    for number in range(species_count):
-        center = conc[number]
-        total = kept * center
-        total = total + weights[0] * layer_above(center)
-        total = total + weights[1] * layer_below(center)
-        for side in range(4):
-            total = total + weights[2 + side] * beside_conc[side, number]
-        moved[number] = total
+    weights[6] = kept
 
     loads[5].wait()
-    chunk = 2
+    chunk = CHUNK
 
     def react_chunk(step, carry):
         span = pl.ds(step * chunk, chunk)
@@ -542,8 +594,15 @@
             [gram_table[max(i, j), min(i, j)] for j in range(mineral_count)]
             for i in range(mineral_count)
         ]
+        scales = [weights[number, span] for number in range(7)]
+        moved = []
+        for c in range(species_count):
+            fields = [conc[c, pl.ds(step * chunk + shift, chunk)] for shift in (2, 0)]
+            fields += [beside_conc[side, c, span] for side in range(4)]
+            fields.append(conc[c, pl.ds(step * chunk + 1, chunk)])
+            moved.append(weighted(scales, fields))
         result = react(
-            [moved[c, span] for c in range(species_count)],
+            moved,
             mineral_zone[span],
             rate_table,
             stoich,
@@ -570,9 +629,8 @@
 
     for copy in halo:
         copy.wait_send()
-    for copy in sends:
-        copy.wait()
-    three = conc.at[pl.ds(0, group * (sp_count - 1))]
+    pltpu.make_async_copy(all_others, all_others, sum_send.at[0]).wait()
+    three = conc.at[pl.ds(0, group * (sp_count - 1)), middle]
     pltpu.make_async_copy(three, three, spread_send.at[0]).wait()
     part = sides_in.at[pl.ds(0, sp_count - 1)]
     pltpu.make_async_copy(part, part, spread_send.at[1]).wait()
@@ -586,7 +644,9 @@
 def hand_over(head, species, head_out, species_out, head_held, species_held, load_sem, store_sem):
     parts = [(head, head_held, head_out)]
     for k in range(species.shape[0]):
-        parts.append((species.at[k], species_held.at[k], species_out.at[k]))
+        for first in range(0, species.shape[1], PIECE):
+            part = (k, pl.ds(first, PIECE))
+            parts.append((species.at[part], species_held.at[part], species_out.at[part]))
     loads, stores = [], []
     for number, (source, held, target) in enumerate(parts):
         loads.append(pltpu.make_async_copy(source, held, load_sem.at[number]))
@@ -637,22 +697,20 @@
                 floats(16, 128),
                 floats(3, 16, 128),
                 floats(gx_count * sp_count, 1, 128),
-                floats(gx_count * sp_count, 1, 128),
-                floats(total, *cells),
+                floats(total, layers + 2, 8, 128),
                 floats(2, group, layers, width),
                 floats(2, total, layers, 128),
                 floats(2 * sp_count, 256),
                 floats(sp_count, 2 * sp_count, 256),
                 floats(4, total, *cells),
-                floats(6, *cells),
-                floats(total, *cells),
+                floats(7, *cells),
                 floats(total, *cells),
                 pltpu.SMEM((minerals, minerals), jnp.float32),
                 pltpu.SemaphoreType.DMA((11,)),
                 pltpu.SemaphoreType.DMA((8,)),
                 pltpu.SemaphoreType.DMA((8,)),
-                pltpu.SemaphoreType.DMA((2,)),
-                pltpu.SemaphoreType.DMA((2,)),
+                pltpu.SemaphoreType.DMA((1,)),
+                pltpu.SemaphoreType.DMA((1,)),
                 pltpu.SemaphoreType.DMA((3,)),
                 pltpu.SemaphoreType.DMA((3,)),
                 pltpu.SemaphoreType.DMA((3,)),
@@ -671,8 +729,8 @@
             out_specs=(hbm, hbm),
             scratch_shapes=[
                 *[floats(*r.shape) for r in results],
-                pltpu.SemaphoreType.DMA((1 + group,)),
-                pltpu.SemaphoreType.DMA((1 + group,)),
+                pltpu.SemaphoreType.DMA((1 + group * layers // PIECE,)),
+                pltpu.SemaphoreType.DMA((1 + group * layers // PIECE,)),
             ],
             compiler_params=pltpu.CompilerParams(vmem_limit_bytes=60 * 1024 * 1024),
         )(*results)

time: 39.2 us -> 34.5 us (0.88)
  Pallas kernels: 38.4 us -> 33.7 us
    pallas_call x1, Pallas kernels: 36.6 us -> 31.9 us  [per_device(): pl.pallas_call(functools.partial(step_kernel, gx_count, sp_count, inner),...]
where the time goes in v6:
time: 34.5 us; the launch traced here: 34.3 us
  Pallas kernels  33.7 us (98%)
  between operations  0.64 us (2%)
    pallas_call x1, Pallas kernels, per_device(): pl.pallas_call(functools.partial(step_kernel, gx_count, sp_count, inner),...  31.9 us
    pallas_call x1, Pallas kernels, per_device(): pl.pallas_call(hand_over, out_shape=tuple((jax.ShapeDtypeStruct(r.shape,...  1.8 us

profile of v6, /device:TPU:1, one launch (start us, length us, event | category | flops | bytes accessed | tf_op | source)
XLA Modules:
  0.0 34.3 jit_solution(781880057261551459)
XLA Ops:
  0.6 31.9 %shard_map.113 = (f32[8,8,128]{2,1,0:T(8,128)}, f32[3,8,8,512]{3,2,1,0:T(8,128)}) custom-call(f32[8,8,128]{2,1,0:T(8,128)} %previous_head_in.1, f32[8,8,128]{2,1,0:T(8,128)} %recharge_in.1, s32[8,8,128]{2,1,0:T(8,128)} %soil_zone_in.1, f32[8]{0:T(128)} %soil_cond_in.1, f32[8]{0:T(128)} %soil_store_in.1, f32[3,8,8,512]{3,2,1,0:T(8,128)} %species_in.1, ...), custom_call_target="tpu_custom_call" | custom-call | tf_op jit(solution)/shard_map/pallas_call | solution.py:680
  32.5 1.8 %shard_map.114 = (f32[8,8,128]{2,1,0:T(8,128)}, f32[3,8,8,512]{3,2,1,0:T(8,128)}) custom-call(f32[8,8,128]{2,1,0:T(8,128)} %get-tuple-element.4.head, f32[3,8,8,512]{3,2,1,0:T(8,128)} %get-tuple-element.5.species), custom_call_target="tpu_custom_call" | custom-call | tf_op jit(solution)/shard_map/pallas_call | solution.py:725

commit v7 on v6

--- a/solution.py
+++ b/solution.py
@@ -8,6 +8,7 @@
 from jax.sharding import PartitionSpec as P
 
 NEWTON = 2
+ROUNDING = 4.3e-12
 SHIFTS = (0.5, 0.125, 1.0, 0.25, 1.0, 0.0625)
 CHUNK = 2
 PIECE = 2
@@ -165,11 +166,18 @@
                 after = pair_add(after, (shift * gram[i, j][0], shift * gram[i, j][1]))
             matrix[j, i] = after
     right = [gram[0, i] for i in range(size)]
-    first = [gram[k, k][0] for k in range(size)]
+    squares = [gram[k, k][0] for k in range(size)]
+    mixes = []
     inverse, lower = [None] * size, {}
     for k in range(size):
         pivot = matrix[k, k]
-        usable = pivot[0] > 8e-12 * first[k]
+        mix = [jnp.zeros_like(squares[0])] * k + [jnp.ones_like(squares[0])]
+        for i in range(k):
+            for j in range(i + 1):
+                mix[j] = mix[j] - lower[k, i][0] * mixes[i][j]
+        mixes.append(mix)
+        noise = weighted([value * value for value in mix], squares)
+        usable = pivot[0] > ROUNDING * noise
         inverse[k] = tuple(jnp.where(usable, part, 0.0) for part in pair_inverse(pivot))
         for i in range(k + 1, size):
             lower[i, k] = pair_times(matrix[i, k], inverse[k])

time: 34.5 us -> 34.5 us (level)
  no operation moved by 1% of the time
where the time goes in v7:
time: 34.5 us; the launch traced here: 34.3 us
  Pallas kernels  33.7 us (98%)
  between operations  0.64 us (2%)
    pallas_call x1, Pallas kernels, per_device(): pl.pallas_call(functools.partial(step_kernel, gx_count, sp_count, inner),...  31.9 us
    pallas_call x1, Pallas kernels, per_device(): pl.pallas_call(hand_over, out_shape=tuple((jax.ShapeDtypeStruct(r.shape,...  1.8 us

profile of v7, /device:TPU:1, one launch (start us, length us, event | category | flops | bytes accessed | tf_op | source)
XLA Modules:
  0.0 34.3 jit_solution(4880574511276532498)
XLA Ops:
  0.6 31.9 %shard_map.113 = (f32[8,8,128]{2,1,0:T(8,128)}, f32[3,8,8,512]{3,2,1,0:T(8,128)}) custom-call(f32[8,8,128]{2,1,0:T(8,128)} %previous_head_in.1, f32[8,8,128]{2,1,0:T(8,128)} %recharge_in.1, s32[8,8,128]{2,1,0:T(8,128)} %soil_zone_in.1, f32[8]{0:T(128)} %soil_cond_in.1, f32[8]{0:T(128)} %soil_store_in.1, f32[3,8,8,512]{3,2,1,0:T(8,128)} %species_in.1, ...), custom_call_target="tpu_custom_call" | custom-call | tf_op jit(solution)/shard_map/pallas_call | solution.py:688
  32.5 1.8 %shard_map.114 = (f32[8,8,128]{2,1,0:T(8,128)}, f32[3,8,8,512]{3,2,1,0:T(8,128)}) custom-call(f32[8,8,128]{2,1,0:T(8,128)} %get-tuple-element.4.head, f32[3,8,8,512]{3,2,1,0:T(8,128)} %get-tuple-element.5.species), custom_call_target="tpu_custom_call" | custom-call | tf_op jit(solution)/shard_map/pallas_call | solution.py:733

commit v8 on v7

--- a/solution.py
+++ b/solution.py
@@ -8,7 +8,7 @@
 from jax.sharding import PartitionSpec as P
 
 NEWTON = 2
-ROUNDING = 4.3e-12
+ROUNDING = 1.7e-13
 SHIFTS = (0.5, 0.125, 1.0, 0.25, 1.0, 0.0625)
 CHUNK = 2
 PIECE = 2
@@ -126,6 +126,28 @@
     half = total.shape[0] // 2
     total, more = exact_sum(total[:half], total[half:])
     return total, error[:half] + error[half:] + more
+
+
+def exact_product(left, left_parts, right):
+    high, low = split(right)
+    product = left * right
+    error = left_parts[0] * high - product
+    error = error + left_parts[0] * low + left_parts[1] * high + left_parts[1] * low
+    return product, error
+
+
+def rounding_left(field, following, shift, scale, factors, beside):
+    total, error = exact_product(*factors[0], field)
+    for factor, other in zip(factors[1:], beside):
+        gap, lost = exact_sum(field, -other)
+        flow, more = exact_product(*factor, gap)
+        total, rest = exact_sum(total, flow)
+        error = error + (rest + (more + factor[0] * lost))
+    scaled, more = exact_product(*scale, total)
+    more = more + scale[0] * error
+    scaled, rest = exact_sum(scaled, -shift * field)
+    left, last = exact_sum(scaled, -following)
+    return left + (last + (rest + more))
 
 
 def inner_product(left, right):
@@ -156,7 +178,7 @@
     return pairs[0]
 
 
-def solve_krylov(gram):
+def solve_krylov(gram, rounding):
     size = len(SHIFTS)
     matrix = {}
     for i in range(size):
@@ -164,6 +186,7 @@
             after = pair_add(gram[i, j + 1], gram[min(i + 1, j), max(i + 1, j)])
             for shift in (SHIFTS[i], SHIFTS[j]):
                 after = pair_add(after, (shift * gram[i, j][0], shift * gram[i, j][1]))
+            after = pair_add(after, (rounding[i, j], jnp.zeros_like(after[0])))
             matrix[j, i] = after
     right = [gram[0, i] for i in range(size)]
     squares = [gram[k, k][0] for k in range(size)]
@@ -541,6 +564,24 @@
         basis.append(image - shift * basis[-1])
     parts = [split(own(vector)) for vector in basis]
     size = len(SHIFTS)
+    factors = [(own(factor), split(own(factor))) for factor in (storage,) + faces]
+    scaling = (scale[:, :128], split(scale[:, :128]))
+    lost = [
+        rounding_left(
+            own(basis[k]),
+            own(basis[k + 1]),
+            SHIFTS[k],
+            scaling,
+            factors,
+            [own(other) for other in six_beside(basis[k])],
+        )
+        for k in range(size)
+    ]
+    corners = [(i, j) for i in range(size) for j in range(i, size)]
+    repairs = []
+    for i, j in corners:
+        product = own(basis[i]) * lost[j] + own(basis[j]) * lost[i]
+        repairs.append(jnp.sum(product, axis=0))
     places = [(i, j) for i in range(size) for j in range(i, size + 1)]
     products = [inner_product(parts[i], parts[j]) for i, j in places]
     lines = 32
@@ -548,6 +589,9 @@
     products += [(blank, blank)] * (lines - len(products))
     rows = [merge_rows(products[first : first + 8]) for first in range(0, lines, 8)]
     rows = [row[0] for row in rows] + [row[1] for row in rows]
+    repairs = [(repair, blank) for repair in repairs]
+    repairs += [(blank, blank)] * (24 - len(repairs))
+    rows += [merge_rows(repairs[first : first + 8])[0] for first in range(0, 24, 8)]
     table = jnp.concatenate(rows + [blank] * (16 - len(rows)), axis=0).T
     error = jnp.zeros_like(table)
     while table.shape[0] > 8:
@@ -556,7 +600,13 @@
         table, more = exact_sum(table, pltpu.roll(table, shift, 0))
         error = error + pltpu.roll(error, shift, 0) + more
     lane = lax.broadcasted_iota(jnp.int32, (8, 128), 1)
-    table = jnp.where(lane < 2 * lines, table, pltpu.roll(error, 2 * lines, 1))
+    table = jnp.where(
+        lane < 2 * lines,
+        table,
+        jnp.where(
+            lane < 3 * lines, pltpu.roll(error, 2 * lines, 1), pltpu.roll(table, lines, 1)
+        ),
+    )
     gathered[slot] = table[:1]
     for peer in everyone:
         remote(gathered.at[slot], gathered.at[slot], sum_send.at[0], sum_recv.at[0], peer)
@@ -571,6 +621,7 @@
     table = jnp.broadcast_to(table[0], (8, 128))
     error = jnp.broadcast_to(error[0], (8, 128))
     error = error + pltpu.roll(table, 128 - 2 * lines, 1) + pltpu.roll(table, 128 - lines, 1)
+    repair = pltpu.roll(table, 128 - 3 * lines, 1)
     high, low = paired(table, error)
     entries = {
         place: tuple(
@@ -578,7 +629,11 @@
         )
         for k, place in enumerate(places)
     }
-    answer = solve_krylov(entries)
+    rounding = {
+        place: jnp.broadcast_to(repair[:1, k : k + 1], (1, 128))
+        for k, place in enumerate(corners)
+    }
+    answer = solve_krylov(entries, rounding)
     head = None
     for value, vector in zip(answer, basis):
         term = (scale * jnp.concatenate([value, value], axis=1))[None] * vector

time: 34.5 us -> 36.1 us (1.046)
  Pallas kernels: 33.7 us -> 35.2 us
    pallas_call x1, Pallas kernels: 31.9 us -> 33.4 us  [per_device(): pl.pallas_call(functools.partial(step_kernel, gx_count, sp_count, inner),...]
where the time goes in v8:
time: 36.1 us; the launch traced here: 35.9 us
  Pallas kernels  35.2 us (98%)
  between operations  0.64 us (2%)
    pallas_call x1, Pallas kernels, per_device(): pl.pallas_call(functools.partial(step_kernel, gx_count, sp_count, inner),...  33.4 us
    pallas_call x1, Pallas kernels, per_device(): pl.pallas_call(hand_over, out_shape=tuple((jax.ShapeDtypeStruct(r.shape,...  1.8 us

profile of v8, /device:TPU:1, one launch (start us, length us, event | category | flops | bytes accessed | tf_op | source)
XLA Modules:
  0.0 35.9 jit_solution(14013478506484102042)
XLA Ops:
  0.6 33.4 %shard_map.113 = (f32[8,8,128]{2,1,0:T(8,128)}, f32[3,8,8,512]{3,2,1,0:T(8,128)}) custom-call(f32[8,8,128]{2,1,0:T(8,128)} %previous_head_in.1, f32[8,8,128]{2,1,0:T(8,128)} %recharge_in.1, s32[8,8,128]{2,1,0:T(8,128)} %soil_zone_in.1, f32[8]{0:T(128)} %soil_cond_in.1, f32[8]{0:T(128)} %soil_store_in.1, f32[3,8,8,512]{3,2,1,0:T(8,128)} %species_in.1, ...), custom_call_target="tpu_custom_call" | custom-call | tf_op jit(solution)/shard_map/pallas_call | solution.py:743
  34.1 1.8 %shard_map.114 = (f32[8,8,128]{2,1,0:T(8,128)}, f32[3,8,8,512]{3,2,1,0:T(8,128)}) custom-call(f32[8,8,128]{2,1,0:T(8,128)} %get-tuple-element.4.head, f32[3,8,8,512]{3,2,1,0:T(8,128)} %get-tuple-element.5.species), custom_call_target="tpu_custom_call" | custom-call | tf_op jit(solution)/shard_map/pallas_call | solution.py:788

commit v9 on v7

--- a/solution.py
+++ b/solution.py
@@ -619,7 +619,7 @@
         )
         for c in range(species_count):
             reacted[c, span] = result[c]
-        for k in range(1, sp_count):
+        for k in sorted(range(1, sp_count), key=lambda k: -hops(k, sp_count)):
             to = (s + k) % sp_count
             remote(
                 reacted.at[pl.ds(group * to, group), span],

time: 34.5 us -> 34.3 us (level)
  no operation moved by 1% of the time
where the time goes in v9:
time: 34.3 us; the launch traced here: 34.1 us
  Pallas kernels  33.4 us (97%)
  between operations  0.64 us (2%)
    pallas_call x1, Pallas kernels, per_device(): pl.pallas_call(functools.partial(step_kernel, gx_count, sp_count, inner),...  31.6 us
    pallas_call x1, Pallas kernels, per_device(): pl.pallas_call(hand_over, out_shape=tuple((jax.ShapeDtypeStruct(r.shape,...  1.8 us

profile of v9, /device:TPU:1, one launch (start us, length us, event | category | flops | bytes accessed | tf_op | source)
XLA Modules:
  0.0 34.1 jit_solution(37549556466248896)
XLA Ops:
  0.6 31.6 %shard_map.113 = (f32[8,8,128]{2,1,0:T(8,128)}, f32[3,8,8,512]{3,2,1,0:T(8,128)}) custom-call(f32[8,8,128]{2,1,0:T(8,128)} %previous_head_in.1, f32[8,8,128]{2,1,0:T(8,128)} %recharge_in.1, s32[8,8,128]{2,1,0:T(8,128)} %soil_zone_in.1, f32[8]{0:T(128)} %soil_cond_in.1, f32[8]{0:T(128)} %soil_store_in.1, f32[3,8,8,512]{3,2,1,0:T(8,128)} %species_in.1, ...), custom_call_target="tpu_custom_call" | custom-call | tf_op jit(solution)/shard_map/pallas_call | solution.py:688
  32.3 1.8 %shard_map.114 = (f32[8,8,128]{2,1,0:T(8,128)}, f32[3,8,8,512]{3,2,1,0:T(8,128)}) custom-call(f32[8,8,128]{2,1,0:T(8,128)} %get-tuple-element.4.head, f32[3,8,8,512]{3,2,1,0:T(8,128)} %get-tuple-element.5.species), custom_call_target="tpu_custom_call" | custom-call | tf_op jit(solution)/shard_map/pallas_call | solution.py:733
